TPU v7x, 32 devices: a whole 2x2x4 slice. The times are simulated.
32 devices in a mesh: dp: 8 (over z, x), head: 4 (over y, core).
Axes of the slice: x: 2, y: 2, z: 4, core: 2. Of those that a mesh axis runs over, the one named last changes fastest.
Arguments:
- layer_input: bfloat16 [32768, 768], P(('dp', 'head')), may hold values from -6 to 6
- out_grad: bfloat16 [32768, 768], P(('dp', 'head'))
- matrices: float32 [3, 768, 3072], P(None, None, ('dp', 'head'))
- mat_first: float32 [3, 768, 3072], P(None, None, ('dp', 'head'))
- mat_second: float32 [3, 768, 3072], P(None, None, ('dp', 'head')), as said below
- mat_ema: float32 [3, 768, 3072], P(None, None, ('dp', 'head'))
- gains: float32 [2, 768], replicated, may hold values from 0.5 to 1.5
- gain_first: float32 [2, 768], replicated
- gain_second: float32 [2, 768], replicated, as said below
- rel_bias: float32 [32, 12], replicated, may hold values from -3 to 3
- bias_first: float32 [32, 12], replicated
- bias_second: float32 [32, 12], replicated, as said below
- bucket_len: int32 [64], P('dp'), may hold values from 128 to 512, as said below
- item_count: int32 [64], P('dp'), may hold values from 1 to 4, as said below
- bucket_table: int32 [1023], replicated, may hold values from 0 to 31, as said below
Outputs:
- layer_output: bfloat16 [32768, 768], P(('dp', 'head'))
- input_grad: float32 [32768, 768], P(('dp', 'head'))
- mat_grad: float32 [3, 768, 3072], P(None, None, ('dp', 'head'))
- mat_new: float32 [3, 768, 3072], P(None, None, ('dp', 'head'))
- mat_first_new: float32 [3, 768, 3072], P(None, None, ('dp', 'head'))
- mat_second_new: float32 [3, 768, 3072], P(None, None, ('dp', 'head'))
- mat_ema_new: float32 [3, 768, 3072], P(None, None, ('dp', 'head'))
- gain_grad: float32 [2, 768], replicated
- gain_new: float32 [2, 768], replicated
- gain_first_new: float32 [2, 768], replicated
- gain_second_new: float32 [2, 768], replicated
- bias_grad: float32 [32, 12], replicated
- bias_new: float32 [32, 12], replicated
- bias_first_new: float32 [32, 12], replicated
- bias_second_new: float32 [32, 12], replicated
Inputs may be any that keep to these rules, and one draw needn't show every extreme that they name: `bucket_len`: every packed row holds items of one length, 128, 256 or 512; some row has length 128 and some row 512. `item_count`: items fill a packed row from its start, at most 512 divided by the row's length of them; the other slots are padding; some row holds 4. `bucket_table`: entry r + 511 is the bucket of relative position r, query position minus key position. `mat_second`: positive. `gain_second`: positive. `bias_second`: positive.
All inputs are finite; a program needn't handle non-finite values.
Results may differ from a plain program's by a relative error of at most 0.014.
The roundings to bfloat16 on the way count: a program that leaves them out, or rounds other values in their place, can miss the bound.
Values may be sent and summed in bfloat16 or wider, within the bound.
No kernel may reach another device: no remote copies, remote signals or barrier semaphores. Data moves between devices by JAX's collectives and lax.ppermute only.
A program may use at most 256 MiB of HBM per device.

v0:
```python
import jax
import jax.numpy as jnp
from jax import lax
from jax.sharding import PartitionSpec as P

D = 768
HEADS = 12
HD = 64
BUCKETS = 32
ROW = 512
STEP = 10


EPS = 1e-06
NEG = -1e30
RATE = 0.05
RATE_SMALL = 0.5
BETA_ONE = 0.9
BETA_TWO = 0.999
ADAM_EPS = 1e-08
DECAY = 0.1
EMA_KEEP = 0.75


def rms_scale(value, gain):
    return value * lax.rsqrt(jnp.mean(value * value, axis=-1, keepdims=True) + EPS) * gain


def smooth_gate(value):
    return 0.5 * value * (1.0 + jnp.tanh(0.7978845608 * (value + 0.044715 * value * value * value)))


def bucket_onehot(bucket_table):
    places = jnp.arange(ROW, dtype=jnp.int32)
    offsets = (places[:, None] - places[None, :] + (ROW - 1)).reshape(-1)
    chosen = jnp.take(bucket_table, offsets)
    return (chosen[None, :] == jnp.arange(BUCKETS, dtype=jnp.int32)[:, None]).astype(jnp.float32)


def row_masks(length, items_in):
    places = jnp.arange(ROW, dtype=jnp.int32)
    live_rows = places < length * items_in
    slots = places // length
    allowed = (slots[:, None] == slots[None, :]) & live_rows[None, :]
    return (allowed, live_rows.astype(jnp.float32))


def scores_of(queries, key_rows, bias_here, allowed):
    scores = (
        jnp.einsum("ihd,jhd->hij", queries, key_rows, preferred_element_type=jnp.float32)
        + bias_here
    )
    return jnp.where(allowed[None], scores, NEG)


def attend(queries, key_rows, values, bias_here, allowed, live_rows):
    scores = scores_of(queries, key_rows, bias_here, allowed)
    row_top = jnp.max(scores, axis=-1, keepdims=True)
    exponent = jnp.exp(scores - row_top)
    row_total = jnp.sum(exponent, axis=-1, keepdims=True)
    attention = exponent / row_total * live_rows[None, :, None]
    mixed_heads = jnp.einsum(
        "hij,jhd->ihd", attention.astype(jnp.bfloat16), values, preferred_element_type=jnp.float32
    )
    return (mixed_heads.astype(jnp.bfloat16), (row_top + jnp.log(row_total))[..., 0])


def attend_back(queries, key_rows, values, bias_here, allowed, live_rows, row_lse, grad_mix):
    scores = scores_of(queries, key_rows, bias_here, allowed)
    softened = jnp.exp(scores - row_lse[..., None])
    live_column = live_rows[None, :, None]
    grad_attention = (
        jnp.einsum("ihd,jhd->hij", grad_mix, values, preferred_element_type=jnp.float32)
        * live_column
    )
    grad_scores = softened * (
        grad_attention - jnp.sum(softened * grad_attention, axis=-1, keepdims=True)
    )
    grad_low = grad_scores.astype(jnp.bfloat16)
    attention_low = (softened * live_column).astype(jnp.bfloat16)
    grad_queries = jnp.einsum(
        "hij,jhd->ihd", grad_low, key_rows, preferred_element_type=jnp.float32
    )
    grad_keys = jnp.einsum("hij,ihd->jhd", grad_low, queries, preferred_element_type=jnp.float32)
    grad_values = jnp.einsum(
        "hij,ihd->jhd", attention_low, grad_mix, preferred_element_type=jnp.float32
    )
    stacked = jnp.stack([grad_queries, grad_keys, grad_values], axis=1).astype(jnp.bfloat16)
    return (stacked, grad_low.astype(jnp.float32))


def adam_update(param, grad, first, second, rate):
    first_new = BETA_ONE * first + (1.0 - BETA_ONE) * grad
    second_new = BETA_TWO * second + (1.0 - BETA_TWO) * grad * grad
    first_hat = first_new / (1.0 - BETA_ONE**STEP)
    second_hat = second_new / (1.0 - BETA_TWO**STEP)
    param_new = param - rate * (first_hat / (jnp.sqrt(second_hat) + ADAM_EPS) + DECAY * param)
    return (param_new, first_new, second_new)


def on_device(
    layer_input,
    out_grad,
    matrices,
    mat_first,
    mat_second,
    mat_ema,
    gains,
    gain_first,
    gain_second,
    rel_bias,
    bias_first,
    bias_second,
    bucket_len,
    item_count,
    bucket_table,
):
    head_groups = lax.axis_size("head")
    heads_here = HEADS // head_groups
    head_start = lax.axis_index("head") * heads_here
    tokens_here = layer_input.shape[0]
    weights_low = matrices.astype(jnp.bfloat16)
    gathered = lax.all_gather(weights_low, ("dp", "head"), axis=2, tiled=True)
    attn_weight = gathered[0]
    qkv_weight = attn_weight[:, : 3 * D]
    out_weight = attn_weight[:, 3 * D :]
    inputs = layer_input.astype(jnp.float32)
    normed, first_back = jax.vjp(rms_scale, inputs, gains[0])
    normed_low = normed.astype(jnp.bfloat16)
    packed = jnp.dot(normed_low, qkv_weight, preferred_element_type=jnp.float32).astype(
        jnp.bfloat16
    )
    by_heads = lax.all_to_all(
        packed.reshape(tokens_here, 3, D), "head", split_axis=2, concat_axis=0, tiled=True
    )
    by_heads = by_heads.reshape(-1, ROW, 3, heads_here, HD)
    onehot = bucket_onehot(bucket_table)
    local_table = lax.dynamic_slice_in_dim(rel_bias, head_start, heads_here, 1)
    bias_here = jnp.dot(local_table.T, onehot, precision=lax.Precision.HIGHEST).reshape(
        heads_here, ROW, ROW
    )

    def forward_row(pieces):
        row_block, length, items_in = pieces
        allowed, live_rows = row_masks(length, items_in)
        return attend(
            row_block[:, 0], row_block[:, 1], row_block[:, 2], bias_here, allowed, live_rows
        )

    mixed_rows, row_lse = lax.map(forward_row, (by_heads, bucket_len, item_count))
    mixed_seq = lax.all_to_all(
        mixed_rows.reshape(-1, heads_here * HD), "head", split_axis=0, concat_axis=1, tiled=True
    )
    middle = inputs + jnp.dot(mixed_seq, out_weight, preferred_element_type=jnp.float32)
    second, second_back = jax.vjp(rms_scale, middle, gains[1])
    second_low = second.astype(jnp.bfloat16)
    up_part = gathered[1]
    down_part = gathered[2]
    pre_act = jnp.dot(second_low, up_part, preferred_element_type=jnp.float32)
    activated, gate_back = jax.vjp(smooth_gate, pre_act)
    hidden = activated.astype(jnp.bfloat16)
    ffn_term = jnp.einsum("tf,df->td", hidden, down_part, preferred_element_type=jnp.float32)
    layer_output = (middle + ffn_term).astype(jnp.bfloat16)
    cotangent = out_grad.astype(jnp.float32)
    grad_down = jnp.einsum("td,tf->df", out_grad, hidden, preferred_element_type=jnp.float32)
    grad_hidden = jnp.dot(out_grad, down_part, preferred_element_type=jnp.float32).astype(
        jnp.bfloat16
    )
    grad_pre = gate_back(grad_hidden.astype(jnp.float32))[0].astype(jnp.bfloat16)
    grad_up = jnp.einsum("td,tf->df", second_low, grad_pre, preferred_element_type=jnp.float32)
    second_part = jnp.einsum("tf,df->td", grad_pre, up_part, preferred_element_type=jnp.float32)
    middle_part, grad_gain_two = second_back(second_part)
    grad_middle = cotangent + middle_part
    grad_branch = grad_middle.astype(jnp.bfloat16)
    grad_out_weight = jnp.einsum(
        "td,te->de", mixed_seq, grad_branch, preferred_element_type=jnp.float32
    )
    grad_mixed = jnp.einsum(
        "te,de->td", grad_branch, out_weight, preferred_element_type=jnp.float32
    ).astype(jnp.bfloat16)
    grad_heads = lax.all_to_all(
        grad_mixed, "head", split_axis=1, concat_axis=0, tiled=True
    ).reshape(-1, ROW, heads_here, HD)

    def backward_row(score_total, pieces):
        row_block, length, items_in, lse_row, grad_row = pieces
        allowed, live_rows = row_masks(length, items_in)
        stacked, grad_scores = attend_back(
            row_block[:, 0],
            row_block[:, 1],
            row_block[:, 2],
            bias_here,
            allowed,
            live_rows,
            lse_row,
            grad_row,
        )
        return (score_total + grad_scores, stacked)

    score_start = jnp.zeros((heads_here, ROW, ROW), jnp.float32)
    score_total, grad_blocks = lax.scan(
        backward_row, score_start, (by_heads, bucket_len, item_count, row_lse, grad_heads)
    )
    grad_packed = lax.all_to_all(
        grad_blocks.reshape(-1, 3, heads_here * HD), "head", split_axis=0, concat_axis=2, tiled=True
    )
    grad_packed = grad_packed.reshape(tokens_here, 3 * D)
    grad_qkv = jnp.einsum("td,te->de", normed_low, grad_packed, preferred_element_type=jnp.float32)
    grad_normed = jnp.einsum(
        "te,de->td", grad_packed, qkv_weight, preferred_element_type=jnp.float32
    )
    input_part, grad_gain_one = first_back(grad_normed)
    input_grad = grad_middle + input_part
    grad_attn = jnp.concatenate([grad_qkv, grad_out_weight], axis=1)[None]
    mat_grad = lax.psum_scatter(
        jnp.concatenate([grad_attn, grad_up[None], grad_down[None]], axis=0),
        ("dp", "head"),
        scatter_dimension=2,
        tiled=True,
    )
    bias_local = jnp.dot(
        onehot, score_total.reshape(heads_here, -1).T, precision=lax.Precision.HIGHEST
    )
    bias_full = lax.dynamic_update_slice(
        jnp.zeros((BUCKETS, HEADS), jnp.float32), bias_local, (0, head_start)
    )
    gain_local = jnp.stack([grad_gain_one, grad_gain_two])
    gain_grad, bias_grad = lax.psum((gain_local, bias_full), ("dp", "head"))
    mat_new, mat_first_new, mat_second_new = adam_update(
        matrices, mat_grad, mat_first, mat_second, RATE
    )
    mat_ema_new = EMA_KEEP * mat_ema + (1.0 - EMA_KEEP) * mat_new
    gain_new, gain_first_new, gain_second_new = adam_update(
        gains, gain_grad, gain_first, gain_second, RATE_SMALL
    )
    bias_new, bias_first_new, bias_second_new = adam_update(
        rel_bias, bias_grad, bias_first, bias_second, RATE_SMALL
    )
    return (
        layer_output,
        input_grad,
        mat_grad,
        mat_new,
        mat_first_new,
        mat_second_new,
        mat_ema_new,
        gain_grad,
        gain_new,
        gain_first_new,
        gain_second_new,
        bias_grad,
        bias_new,
        bias_first_new,
        bias_second_new,
    )


def solution(mesh):
    placed = (
        P(("dp", "head"), None),
        P(("dp", "head"), None),
        P(None, None, ("dp", "head")),
        P(None, None, ("dp", "head")),
        P(None, None, ("dp", "head")),
        P(None, None, ("dp", "head")),
        P(),
        P(),
        P(),
        P(),
        P(),
        P(),
        P("dp"),
        P("dp"),
        P(),
    )
    return jax.shard_map(
        on_device,
        mesh=mesh,
        in_specs=placed,
        out_specs=(
            P(("dp", "head"), None),
            P(("dp", "head"), None),
            P(None, None, ("dp", "head")),
            P(None, None, ("dp", "head")),
            P(None, None, ("dp", "head")),
            P(None, None, ("dp", "head")),
            P(None, None, ("dp", "head")),
            P(),
            P(),
            P(),
            P(),
            P(),
            P(),
            P(),
            P(),
        ),
        check_vma=False,
    )
```

profile of v0, /device:TPU:0, one launch (start us, length us, event | category | flops | bytes accessed | tf_op | source)
XLA Modules:
  0.0 3088.3 jit_solution(10033868944875378508)
XLA Ops:
  17.9 2125.1 %gather_fusion = s32[262144]{0:T(1024)} fusion(s32[1023]{0:T(1024)S(1)} %copy-done, s32[262144]{0:T(1024)S(1)} %broadcast_clamp_fusion), kind=kCustom, calls=%fused_computation | custom fusion | bytes 3145728 | tf_op jit(solution)/shard_map/jit(_take)/gather | solution.py:36
  2148.3 6.1 convolution_convert_fusion.2
  2154.4 6.6 copy.182
  2161.0 9.0 copy.183
  2170.1 5.9 all-to-all-start
  2177.2 11.4 fusion.23
  2193.6 53.8 %all-to-all-done = bf16[1024,3,768]{0,1,2:T(4,128)(2,1)} async-done(((bf16[1024,3,768]{0,1,2:T(4,128)(2,1)}), bf16[1024,3,768]{0,1,2:T(4,128)(2,1)}, u32[]{:S(2)}, u32[]{:S(2)}) %all-to-all-start) | async-done | bytes 4718624 | tf_op jit(solution)/shard_map/all_to_all | solution.py:133
  2247.4 4.7 copy.184
  2252.0 5.9 copy.185
  2257.9 7.9 reshape.423
  2265.8 6.1 copy.186
  2271.9 64.5 %while.29 = (s32[]{:T(128)}, bf16[8,512,3,64]{1,3,2,0:T(8,128)(2,1)}, f32[8,3,512]{2,1,0:T(4,128)S(1)}, bf16[8,512,3,3,64]{1,4,3,2,0:T(8,128)(2,1)}, s32[8]{0:T(...) while((s32[]{:T(128)}, bf16[8,512,3,64]{1,3,2,0:T(8,128)(2,1)}, ...), condition=%wide.region_4.5_spmd, body=%wide.region_1.4_spmd.sunk | while | flops 209030656 | bytes 15142049 | solution.py:150
  2336.5 3.4 copy.188
  2339.9 3.7 all_to_all.51
  2346.6 4.4 all-to-all-start.1
  2353.6 17.6 all-to-all-done.1
  2371.1 3.7 multiply_reduce_fusion.3
  2374.8 11.9 fusion.36
  2386.8 16.3 fusion.30
  2403.1 10.0 multiply_reduce_fusion.1
  2414.0 4.8 convolution_convert_fusion.3
  2418.7 4.7 all-to-all-start.2
  2423.5 20.1 all-to-all-done.2
  2443.6 3.8 copy.193
  2447.4 3.5 reshape.425
  2453.9 110.8 %while.30 = (s32[]{:T(128)}, f32[3,512,512]{1,2,0:T(8,128)}, bf16[8,512,3,3,64]{1,4,3,2,0:T(8,128)(2,1)}, s32[8]{0:T(128)S(1)}, s32[8]{0:T(128)S(1)}, /*index=5*...) while((s32[]{:T(128)}, f32[3,512,512]{1,2,0:T(8,128)}, ...), condition=%wide.region_9.10_spmd.clone, body=%wide.region_7.9_spmd.clone.sunk | while | flops 517705216 | bytes 63091968 | solution.py:201
  2564.7 7.4 copy.197
  2572.1 8.3 reshape.426
  2580.4 12.7 copy.198
  2593.1 5.9 all-to-all-start.3
  2599.1 4.5 fusion.58
  2603.6 10.8 convolution_bitcast_fusion.1
  2614.5 8.0 convolution_bitcast_fusion
  2622.5 69.7 %all-to-all-done.3 = bf16[4096,3,192]{2,1,0:T(4,128)(2,1)} async-done(((bf16[4096,3,192]{2,1,0:T(4,128)(2,1)}), bf16[4096,3,192]{2,1,0:T(4,128)(2,1)}, u32[]{:S(2)}, u32[]{:S(2)}) %all-to-all-start.3) | async-done | bytes 4718624 | tf_op jit(solution)/shard_map/all_to_all | solution.py:204
  2692.2 12.9 copy.200
  2705.1 8.3 fusion.61
  2713.5 8.8 maximum_bitcast_fusion
  2722.2 21.1 pad_maximum_fusion
  2743.4 39.0 %copy.224 = f32[3,768,3072]{1,0,2:T(4,128)} copy(f32[3,768,3072]{2,1,0:T(8,128)} %pad_maximum_fusion) | data formatting | bytes 56623104
  2782.4 27.1 copy.232
  2811.4 11.0 add_convert_fusion
  2828.2 4.5 copy.233
  2832.8 16.1 fusion.22
  2849.0 8.2 fusion.41
  2859.8 4.0 copy.211
  2863.9 42.9 %all-reduce = (f32[2,768]{1,0:T(2,128)S(1)}, f32[32,12]{0,1:T(8,128)S(1)}) all-reduce(f32[2,768]{1,0:T(2,128)S(1)} %pad_maximum_fusion.1, f32[32,12]{0,1:T(8,128)S(1)} %dynamic_update_slice.24), channel_id=1, replica_groups=mesh['dp'=8,'head'=4] {'dp','head'}, use_global_device_ids=true, to_apply=%region_14.15 | all-reduce | flops 1920 | bytes 15360 | tf_op jit(solution)/shard_map/psum | solution.py:228
  2908.1 167.5 %reduce-scatter.4.cloned.1.call-done = f32[96,2304]{1,0:T(8,128)} async-done(((f32[3072,2304]{1,0:T(8,128)}), f32[96,2304]{1,0:T(8,128)}) %reduce-scatter.4.cloned.1.call-update) | async-done | bytes 884752
  3077.2 4.0 multiply_add_fusion.2
  (361 shorter events, 188.1 us)
Async XLA Ops:
  7.2 10.6 copy-start
  7.2 2136.2 %all-gather.2.cloned.1.call-start = ((), (), s32[]{:S(2)}) async-start(), calls=%async_computation.5 | async-start | bytes 14598144 | tf_op jit(solution)/shard_map/all_gather | solution.py:123
  13.2 2.8 copy-start.20
  17.8 2125.1 %copy-start.27 = (f32[2,768]{1,0:T(2,128)S(1)}, f32[2,768]{1,0:T(2,128)}, u32[]{:S(2)}) copy-start(f32[2,768]{1,0:T(2,128)} %param.25) | copy-start | bytes 18436
  17.8 2125.1 %copy-start.5 = (bf16[1024,768]{0,1:T(8,128)(2,1)S(1)}, bf16[1024,768]{0,1:T(8,128)(2,1)}, u32[]{:S(2)}) copy-start(bf16[1024,768]{0,1:T(8,128)(2,1)} %copy.181) | copy-start | bytes 4718596
  2143.0 3.1 copy-start.29
  2143.4 2.7 copy-start.31
  2170.1 5.9 copy-start.13
  2170.1 5.9 copy-start.14
  2170.1 6.0 copy-start.15
  2170.1 77.3 %all-to-all-start = ((bf16[1024,3,768]{0,1,2:T(4,128)(2,1)}), bf16[1024,3,768]{0,1,2:T(4,128)(2,1)}, u32[]{:S(2)}, u32[]{:S(2)}) async-start(bf16[1024,3,768]{0,1,2:T(4,128)(2,1)} %copy.183), calls=%async_computation | async-start | bytes 12582912 | tf_op jit(solution)/shard_map/all_to_all | solution.py:133
  2265.8 6.1 copy-start.41
  2265.8 6.1 copy-start.42
  2346.6 24.5 all-to-all-start.1
  2374.8 38.4 %copy-start.17 = (f32[1024,768]{0,1:T(8,128)}, f32[1024,768]{0,1:T(8,128)S(1)}, u32[]{:S(2)}) copy-start(f32[1024,768]{0,1:T(8,128)S(1)} %get-tuple-element.470) | copy-start | bytes 9437188
  2374.8 11.9 copy-start.21
  2403.1 10.1 copy-start.43
  2403.1 10.1 copy-start.11
  2414.0 4.8 copy-start.8
  2418.7 24.9 all-to-all-start.2
  2593.1 6.0 copy-start.9
  2593.1 99.1 %all-to-all-start.3 = ((bf16[4096,3,192]{2,1,0:T(4,128)(2,1)}), bf16[4096,3,192]{2,1,0:T(4,128)(2,1)}, u32[]{:S(2)}, u32[]{:S(2)}) async-start(bf16[4096,3,192]{2,1,0:T(4,128)(2,1)} %copy.198), calls=%async_computation.3 | async-start | bytes 16777216 | tf_op jit(solution)/shard_map/all_to_all | solution.py:204
  2599.0 476.5 %reduce-scatter.4.cloned.1.call-start = ((), (), s32[]{:S(2)}) async-start(), calls=%async_computation.6 | async-start | bytes 29196288
  2599.1 4.5 copy-start.18
  2599.1 15.3 slice-start
  2599.1 15.3 slice-start.1
  2603.6 10.9 copy-start.22
  2603.6 10.9 slice-start.2
  2692.2 12.9 copy-start.6
  2692.2 12.9 copy-start.30
  2692.2 12.9 copy-start.32
  2811.4 13.9 copy-start.40
  2822.4 3.5 copy-start.4
  2828.2 4.5 copy-start.23
  2832.8 16.2 copy-start.7
  2849.0 8.2 copy-start.26
  2849.0 8.3 copy-start.10
  2859.7 47.1 %copy-start.28 = (f32[2,768]{1,0:T(2,128)S(1)}, f32[2,768]{1,0:T(2,128)}, u32[]{:S(2)}) copy-start(f32[2,768]{1,0:T(2,128)} %param.25) | copy-start | bytes 18436
  2859.7 47.1 %copy-start.37 = (f32[2,768]{1,0:T(2,128)S(1)}, f32[2,768]{1,0:T(2,128)}, u32[]{:S(2)}) copy-start(f32[2,768]{1,0:T(2,128)} %param.26) | copy-start | bytes 18436
  2859.7 47.1 %copy-start.38 = (f32[2,768]{1,0:T(2,128)S(1)}, f32[2,768]{1,0:T(2,128)}, u32[]{:S(2)}) copy-start(f32[2,768]{1,0:T(2,128)} %param.27) | copy-start | bytes 18436
  2859.7 47.7 %copy-start.33 = (f32[32,12]{0,1:T(8,128)S(1)}, f32[32,12]{0,1:T(8,128)}, u32[]{:S(2)}) copy-start(f32[32,12]{0,1:T(8,128)} %param.28) | copy-start | bytes 4612
  2859.7 47.7 %copy-start.34 = (f32[32,12]{0,1:T(8,128)S(1)}, f32[32,12]{0,1:T(8,128)}, u32[]{:S(2)}) copy-start(f32[32,12]{0,1:T(8,128)} %param.29) | copy-start | bytes 4612
  2859.8 47.7 %copy-start.35 = (f32[32,12]{0,1:T(8,128)S(1)}, f32[32,12]{0,1:T(8,128)}, u32[]{:S(2)}) copy-start(f32[32,12]{0,1:T(8,128)} %param.30) | copy-start | bytes 4612
  2859.8 217.4 %copy-start.16 = (f32[3,768,96]{1,2,0:T(8,128)S(1)}, f32[3,768,96]{1,2,0:T(8,128)}, u32[]{:S(2)}) copy-start(f32[3,768,96]{1,2,0:T(8,128)} %param.21) | copy-start | bytes 2654212
  2859.8 217.4 %copy-start.24 = (f32[3,768,96]{1,2,0:T(8,128)S(1)}, f32[3,768,96]{1,2,0:T(8,128)}, u32[]{:S(2)}) copy-start(f32[3,768,96]{1,2,0:T(8,128)} %param.24) | copy-start | bytes 2654212
  2906.8 174.3 %copy-start.36 = (f32[32,12]{0,1:T(8,128)}, f32[32,12]{0,1:T(8,128)S(1)}, u32[]{:S(2)}) copy-start(f32[32,12]{0,1:T(8,128)S(1)} %get-tuple-element.447) | copy-start | bytes 4612
  2906.8 174.3 %copy-start.39 = (f32[2,768]{1,0:T(2,128)}, f32[2,768]{1,0:T(2,128)S(1)}, u32[]{:S(2)}) copy-start(f32[2,768]{1,0:T(2,128)S(1)} %get-tuple-element.446) | copy-start | bytes 18436
  3077.1 4.0 copy-start.1
  (19 other events, 38.2 us)
Sparse Core Ops, SparseCore 0:
  11.5 105.9 all-gather.1
  2809.6 265.8 reduce-scatter.3
where the time goes:
time: 3100 us; the launch traced here: 3090 us
  local copies, waits for them, and re-layouts  2370 us (76%)
  waiting for transfers between devices  329 us (11%)
  matrix products  194 us (6%)
  other arithmetic  85.1 us (3%)
  blocking collectives  42.9 us (1%)
  loops' own time  32.1 us (1%)
    gather x1, local copies, waits for them, and re-layouts, bucket_onehot(): chosen = jnp.take(bucket_table, offsets)  2130 us
    unnamed x3, waiting for transfers between devices  167 us
    unnamed x104, local copies, waits for them, and re-layouts  98.7 us
    all_to_all x1, waiting for transfers between devices, on_device(): lax.all_to_all(grad_blocks.reshape(-1, 3, heads_here * HD), 'head', split...  69.7 us
  transfers between devices with their start and end apart: 6, of which 5 were waited for; matrix products, arithmetic and copies ran while one was open for 72% of the time, Pallas kernels for 0%

commit v1 on v0

v1 whole, which is shorter than its diff:
```python
import functools

import jax
import jax.numpy as jnp
from jax import lax
from jax.experimental import pallas as pl
from jax.experimental.pallas import tpu as pltpu
from jax.sharding import Mesh, PartitionSpec as P

D = 768
FF = 3072
HEADS = 12
HD = 64
BUCKETS = 32
ROW = 512
STEP = 10
PAIRS = HEADS // 2
WIDE = 2 * HD
SUB = 128
SPAN = 1024
TOEP = 896

EPS = 1e-06
RATE = 0.05
RATE_SMALL = 0.5
BETA_ONE = 0.9
BETA_TWO = 0.999
ADAM_EPS = 1e-08
DECAY = 0.1
EMA_KEEP = 0.75

F32 = jnp.float32
BF16 = jnp.bfloat16
VMEM_LIMIT = 56 * 1024 * 1024
TILE = 256

NN = (((1,), (0,)), ((), ()))
NT = (((1,), (1,)), ((), ()))
TN = (((0,), (0,)), ((), ()))


def dot(left, right, dims):
    return lax.dot_general(left, right, dims, preferred_element_type=F32)


def params(**more):
    return pltpu.CompilerParams(vmem_limit_bytes=VMEM_LIMIT, **more)


def cost(flops, moved, special=0):
    return pl.CostEstimate(flops=int(flops), bytes_accessed=int(moved), transcendentals=int(special))


def whole(shape):
    return pl.BlockSpec(shape, lambda *_: (0,) * len(shape))


def tiles(rows, columns):
    return pl.BlockSpec((rows, columns), lambda i: (i, 0))


def qkv_kernel(x_ref, gain_ref, weight_ref, normed_ref, packed_ref):
    x = x_ref[...].astype(F32)
    scale = lax.rsqrt(jnp.mean(x * x, axis=-1, keepdims=True) + EPS)
    normed = (x * scale * gain_ref[...]).astype(BF16)
    normed_ref[...] = normed
    for part in range(3):
        cols = slice(part * D, (part + 1) * D)
        packed_ref[:, cols] = dot(normed, weight_ref[cols, :], NT).astype(BF16)


def qkv_call(x, gain, weight):
    tokens = x.shape[0]
    return pl.pallas_call(
        qkv_kernel,
        grid=(tokens // TILE,),
        in_specs=[tiles(TILE, D), whole((1, D)), whole((3 * D, D))],
        out_specs=[tiles(TILE, D), tiles(TILE, 3 * D)],
        out_shape=[
            jax.ShapeDtypeStruct((tokens, D), BF16),
            jax.ShapeDtypeStruct((tokens, 3 * D), BF16),
        ],
        compiler_params=params(),
        cost_estimate=cost(2 * tokens * D * 3 * D, 16e6),
        name="norm_qkv",
    )(x, gain, weight)


def fill_toeplitz(table_ref, toep):
    for h in range(2):
        line = jnp.broadcast_to(table_ref[0, h : h + 1, :], (SUB, SPAN))
        rolled = pltpu.roll(line, SPAN - (SUB - 1), 1, stride=1, stride_axis=0)
        toep[h] = rolled[:, :TOEP]


def head_masks():
    lane = lax.broadcasted_iota(jnp.int32, (1, WIDE), 1)
    return [(lane < HD).astype(BF16), (lane >= HD).astype(BF16)]


def bias_block(toep, h, first, rows, span):
    parts = []
    for t in range(rows // SUB):
        left = ROW - SUB - first - t * SUB
        parts.append(toep[h, :, left : left + span])
    return parts[0] if len(parts) == 1 else jnp.concatenate(parts, axis=0)


def for_items(length, count, body):
    @pl.when(length == ROW)
    def _():
        for first in range(0, ROW, 2 * SUB):
            body(0, first, 2 * SUB, ROW)

    @pl.when(length == ROW // 2)
    def _():
        @pl.loop(0, count)
        def _(item):
            body(item * (ROW // 2), 0, ROW // 2, ROW // 2)

    @pl.when(length == ROW // 4)
    def _():
        @pl.loop(0, count)
        def _(item):
            body(item * (ROW // 4), 0, ROW // 4, ROW // 4)


def aligned(start):
    return start if isinstance(start, int) else pl.multiple_of(start, SUB)


def attend_kernel(len_ref, count_ref, q_ref, k_ref, v_ref, table_ref, o_ref, lse_ref, toep):
    row = pl.program_id(1)

    @pl.when(row == 0)
    def _():
        fill_toeplitz(table_ref, toep)

    length = len_ref[row]
    count = count_ref[row]
    masks = head_masks()

    @pl.when(length * count < ROW)
    def _():
        o_ref[...] = jnp.zeros_like(o_ref)
        lse_ref[...] = jnp.zeros_like(lse_ref)

    def body(start, first, rows, span):
        keys_at = pl.ds(aligned(start), span)
        rows_at = pl.ds(aligned(start + first), rows)
        q = q_ref[rows_at, :]
        k = k_ref[keys_at, :]
        v = v_ref[keys_at, :]
        mixed = None
        stats = []
        for h in range(2):
            s = dot(q, k * masks[h], NT) + bias_block(toep, h, first, rows, span)
            top = jnp.max(s, axis=-1, keepdims=True)
            e = jnp.exp(s - top)
            total = jnp.sum(e, axis=-1, keepdims=True)
            p = (e * (1.0 / total)).astype(BF16)
            part = dot(p, v * masks[h], NN)
            mixed = part if mixed is None else mixed + part
            stats.append(jnp.broadcast_to(top + jnp.log(total), (rows, HD)))
        o_ref[rows_at, :] = mixed.astype(BF16)
        lse_ref[rows_at, :] = jnp.concatenate(stats, axis=1)

    for_items(length, count, body)


def pair_blocks(offset):
    return pl.BlockSpec((ROW, WIDE), lambda p, r, *_: (r, offset + p))


def attend_call(lengths, counts, packed, table):
    tokens = packed.shape[0]
    rows = tokens // ROW
    return pl.pallas_call(
        attend_kernel,
        grid_spec=pltpu.PrefetchScalarGridSpec(
            num_scalar_prefetch=2,
            grid=(PAIRS, rows),
            in_specs=[
                pair_blocks(0),
                pair_blocks(PAIRS),
                pair_blocks(2 * PAIRS),
                pl.BlockSpec((1, 2, SPAN), lambda p, r, *_: (p, 0, 0)),
            ],
            out_specs=[pair_blocks(0), pair_blocks(0)],
            scratch_shapes=[pltpu.VMEM((2, SUB, TOEP), F32)],
        ),
        out_shape=[
            jax.ShapeDtypeStruct((tokens, D), BF16),
            jax.ShapeDtypeStruct((tokens, D), F32),
        ],
        compiler_params=params(),
        cost_estimate=cost(12e9, 10e6, 7e6),
        name="attend",
    )(lengths, counts, packed, packed, packed, table)


def fold_diagonals(grid):
    height = SUB
    total = jnp.concatenate([grid, jnp.zeros((SUB, SPAN - TOEP), F32)], axis=1)
    while height > 8:
        height //= 2
        total = pltpu.roll(total[:height], height, 1) + total[height:]
    line = total[7:8]
    for r in range(7):
        line = line + pltpu.roll(total, 7 - r, 1)[r : r + 1]
    return line


def attend_back_kernel(
    len_ref, count_ref, q_ref, k_ref, v_ref, do_ref, lse_ref, table_ref,
    dq_ref, dk_ref, dv_ref, dbias_ref, toep, diag, dk_acc, dv_acc,
):
    row = pl.program_id(1)

    @pl.when(row == 0)
    def _():
        fill_toeplitz(table_ref, toep)
        diag[...] = jnp.zeros_like(diag)

    length = len_ref[row]
    count = count_ref[row]
    masks = head_masks()

    @pl.when(length * count < ROW)
    def _():
        dq_ref[...] = jnp.zeros_like(dq_ref)
        dk_ref[...] = jnp.zeros_like(dk_ref)
        dv_ref[...] = jnp.zeros_like(dv_ref)

    def body(start, first, rows, span):
        keys_at = pl.ds(aligned(start), span)
        rows_at = pl.ds(aligned(start + first), rows)
        q = q_ref[rows_at, :]
        do = do_ref[rows_at, :]
        k = k_ref[keys_at, :]
        v = v_ref[keys_at, :]
        dq = dk = dv = None
        for h in range(2):
            kh = k * masks[h]
            lse = lse_ref[rows_at, h * HD : h * HD + 1]
            s = dot(q, kh, NT) + bias_block(toep, h, first, rows, span)
            p = jnp.exp(s - lse)
            dp = dot(do, v * masks[h], NT)
            t = p * dp
            ds = t - p * jnp.sum(t, axis=-1, keepdims=True)
            for sub in range(rows // SUB):
                left = ROW - SUB - first - sub * SUB
                diag[h, :, left : left + span] += ds[sub * SUB : (sub + 1) * SUB]
            low = ds.astype(BF16)
            parts = (
                dot(low, kh, NN),
                dot(low, q * masks[h], TN),
                dot(p.astype(BF16), do * masks[h], TN),
            )
            if dq is None:
                dq, dk, dv = parts
            else:
                dq, dk, dv = dq + parts[0], dk + parts[1], dv + parts[2]
        dq_ref[rows_at, :] = dq.astype(BF16)
        if rows == span:
            dk_ref[keys_at, :] = dk.astype(BF16)
            dv_ref[keys_at, :] = dv.astype(BF16)
        elif first == 0:
            dk_acc[...] = dk
            dv_acc[...] = dv
        else:
            dk_ref[...] = (dk_acc[...] + dk).astype(BF16)
            dv_ref[...] = (dv_acc[...] + dv).astype(BF16)

    for_items(length, count, body)

    @pl.when(row == pl.num_programs(1) - 1)
    def _():
        for h in range(2):
            dbias_ref[0, h : h + 1, :] = fold_diagonals(diag[h])


def attend_back_call(lengths, counts, packed, grad_mixed, lse, table):
    tokens = packed.shape[0]
    rows = tokens // ROW
    low = jax.ShapeDtypeStruct((tokens, D), BF16)
    table_block = pl.BlockSpec((1, 2, SPAN), lambda p, r, *_: (p, 0, 0))
    return pl.pallas_call(
        attend_back_kernel,
        grid_spec=pltpu.PrefetchScalarGridSpec(
            num_scalar_prefetch=2,
            grid=(PAIRS, rows),
            in_specs=[
                pair_blocks(0),
                pair_blocks(PAIRS),
                pair_blocks(2 * PAIRS),
                pair_blocks(0),
                pair_blocks(0),
                table_block,
            ],
            out_specs=[pair_blocks(0), pair_blocks(0), pair_blocks(0), table_block],
            scratch_shapes=[
                pltpu.VMEM((2, SUB, TOEP), F32),
                pltpu.VMEM((2, SUB, TOEP), F32),
                pltpu.VMEM((ROW, WIDE), F32),
                pltpu.VMEM((ROW, WIDE), F32),
            ],
        ),
        out_shape=[low, low, low, jax.ShapeDtypeStruct((PAIRS, 2, SPAN), F32)],
        compiler_params=params(),
        cost_estimate=cost(30e9, 16e6, 7e6),
        name="attend_back",
    )(lengths, counts, packed, packed, packed, grad_mixed, lse, table)


def middle_kernel(x_ref, mixed_ref, gain_ref, weight_ref, middle_ref, second_ref):
    middle = x_ref[...].astype(F32) + dot(mixed_ref[...], weight_ref[...], NT)
    middle_ref[...] = middle
    scale = lax.rsqrt(jnp.mean(middle * middle, axis=-1, keepdims=True) + EPS)
    second_ref[...] = (middle * scale * gain_ref[...]).astype(BF16)


def middle_call(x, mixed, gain, weight):
    tokens = x.shape[0]
    return pl.pallas_call(
        middle_kernel,
        grid=(tokens // TILE,),
        in_specs=[tiles(TILE, D), tiles(TILE, D), whole((1, D)), whole((D, D))],
        out_specs=[tiles(TILE, D), tiles(TILE, D)],
        out_shape=[
            jax.ShapeDtypeStruct((tokens, D), F32),
            jax.ShapeDtypeStruct((tokens, D), BF16),
        ],
        compiler_params=params(),
        cost_estimate=cost(2 * tokens * D * D, 9e6),
        name="middle",
    )(x, mixed, gain, weight)


def feed_kernel(second_ref, grad_ref, up_ref, down_ref, out_ref, back_ref, gup_ref, gdown_ref, hidden, dpre):
    step = pl.program_id(0)
    tokens = second_ref.shape[0]

    @pl.when(step == 0)
    def _():
        out_ref[...] = jnp.zeros_like(out_ref)
        back_ref[...] = jnp.zeros_like(back_ref)

    up = up_ref[...]
    down = down_ref[...]

    @pl.loop(0, tokens // TILE)
    def _(tile):
        at = pl.ds(pl.multiple_of(tile * TILE, TILE), TILE)
        u = dot(second_ref[at, :], up, NT)
        square = u * u
        t = jnp.tanh(0.7978845608 * u * (1.0 + 0.044715 * square))
        plus = 0.5 * (1.0 + t)
        low = (u * plus).astype(BF16)
        slope = plus + (0.5 * 0.7978845608) * u * (1.0 - t * t) * (1.0 + 3 * 0.044715 * square)
        dh = dot(grad_ref[at, :], down, NT).astype(BF16).astype(F32)
        du = (dh * slope).astype(BF16)
        hidden[at, :] = low
        dpre[at, :] = du
        out_ref[at, :] += dot(low, down, NN)
        back_ref[at, :] += dot(du, up, NN)

    gdown_ref[...] = dot(hidden[...], grad_ref[...], TN)
    gup_ref[...] = dot(dpre[...], second_ref[...], TN)


def feed_call(second, out_grad, up, down, chunk=384):
    tokens = second.shape[0]
    units = up.shape[0]
    acc = jax.ShapeDtypeStruct((tokens, D), F32)
    grad = jax.ShapeDtypeStruct((units, D), F32)
    return pl.pallas_call(
        feed_kernel,
        grid=(units // chunk,),
        in_specs=[whole((tokens, D)), whole((tokens, D)), tiles(chunk, D), tiles(chunk, D)],
        out_specs=[whole((tokens, D)), whole((tokens, D)), tiles(chunk, D), tiles(chunk, D)],
        out_shape=[acc, acc, grad, grad],
        scratch_shapes=[pltpu.VMEM((tokens, chunk), BF16), pltpu.VMEM((tokens, chunk), BF16)],
        compiler_params=params(),
        cost_estimate=cost(12 * tokens * units * D, 40e6, tokens * units),
        name="feed",
    )(second, out_grad, up, down)


def middle_back_kernel(
    part_ref, middle_ref, grad_ref, mixed_ref, gain_ref, weight_ref,
    dmiddle_ref, dmixed_ref, dgain_ref, dweight_ref,
):
    step = pl.program_id(0)
    db = part_ref[...]
    middle = middle_ref[...]
    scale = lax.rsqrt(jnp.mean(middle * middle, axis=-1, keepdims=True) + EPS)
    dn = db * gain_ref[...]
    inner = jnp.mean(dn * middle, axis=-1, keepdims=True)
    dmiddle = grad_ref[...].astype(F32) + scale * dn - middle * (scale * scale * scale * inner)
    dmiddle_ref[...] = dmiddle
    low = dmiddle.astype(BF16)
    dmixed_ref[...] = dot(low, weight_ref[...], NN).astype(BF16)
    dgain = jnp.sum(db * middle * scale, axis=0, keepdims=True)
    dweight = dot(low, mixed_ref[...], TN)

    @pl.when(step == 0)
    def _():
        dgain_ref[...] = dgain
        dweight_ref[...] = dweight

    @pl.when(step > 0)
    def _():
        dgain_ref[...] += dgain
        dweight_ref[...] += dweight


def middle_back_call(part, middle, out_grad, mixed, gain, weight):
    tokens = part.shape[0]
    return pl.pallas_call(
        middle_back_kernel,
        grid=(tokens // TILE,),
        in_specs=[tiles(TILE, D)] * 4 + [whole((1, D)), whole((D, D))],
        out_specs=[tiles(TILE, D), tiles(TILE, D), whole((1, D)), whole((D, D))],
        out_shape=[
            jax.ShapeDtypeStruct((tokens, D), F32),
            jax.ShapeDtypeStruct((tokens, D), BF16),
            jax.ShapeDtypeStruct((1, D), F32),
            jax.ShapeDtypeStruct((D, D), F32),
        ],
        compiler_params=params(),
        cost_estimate=cost(4 * tokens * D * D, 18e6),
        name="middle_back",
    )(part, middle, out_grad, mixed, gain, weight)


def qkv_grad_kernel(dq_ref, dk_ref, dv_ref, normed_ref, out_ref):
    step = pl.program_id(0)
    for part, ref in enumerate((dq_ref, dk_ref, dv_ref)):

        @pl.when(step // 2 == part)
        def _(ref=ref):
            out_ref[...] = dot(ref[...], normed_ref[...], TN)


def qkv_grad_call(dq, dk, dv, normed):
    tokens = normed.shape[0]
    half = D // 2

    def columns(part):
        return pl.BlockSpec((tokens, half), lambda i: (0, jnp.clip(i - 2 * part, 0, 1)))

    return pl.pallas_call(
        qkv_grad_kernel,
        grid=(6,),
        in_specs=[columns(0), columns(1), columns(2), whole((tokens, D))],
        out_specs=tiles(half, D),
        out_shape=jax.ShapeDtypeStruct((3 * D, D), F32),
        compiler_params=params(),
        cost_estimate=cost(2 * tokens * D * 3 * D, 16e6),
        name="qkv_grad",
    )(dq, dk, dv, normed)


def input_back_kernel(dq_ref, dk_ref, dv_ref, x_ref, dmiddle_ref, gain_ref, weight_ref, dx_ref, dgain_ref):
    step = pl.program_id(0)
    da = dot(dq_ref[...], weight_ref[:D, :], NN)
    da += dot(dk_ref[...], weight_ref[D : 2 * D, :], NN)
    da += dot(dv_ref[...], weight_ref[2 * D :, :], NN)
    x = x_ref[...].astype(F32)
    scale = lax.rsqrt(jnp.mean(x * x, axis=-1, keepdims=True) + EPS)
    dm = da * gain_ref[...]
    inner = jnp.mean(dm * x, axis=-1, keepdims=True)
    dx_ref[...] = dmiddle_ref[...] + scale * dm - x * (scale * scale * scale * inner)
    dgain = jnp.sum(da * x * scale, axis=0, keepdims=True)

    @pl.when(step == 0)
    def _():
        dgain_ref[...] = dgain

    @pl.when(step > 0)
    def _():
        dgain_ref[...] += dgain


def input_back_call(dq, dk, dv, x, dmiddle, gain, weight):
    tokens = x.shape[0]
    return pl.pallas_call(
        input_back_kernel,
        grid=(tokens // TILE,),
        in_specs=[tiles(TILE, D)] * 5 + [whole((1, D)), whole((3 * D, D))],
        out_specs=[tiles(TILE, D), whole((1, D))],
        out_shape=[jax.ShapeDtypeStruct((tokens, D), F32), jax.ShapeDtypeStruct((1, D), F32)],
        compiler_params=params(),
        cost_estimate=cost(2 * tokens * D * 3 * D, 18e6),
        name="input_back",
    )(dq, dk, dv, x, dmiddle, gain, weight)


def adam_update(param, grad, first, second, rate):
    first_new = BETA_ONE * first + (1.0 - BETA_ONE) * grad
    second_new = BETA_TWO * second + (1.0 - BETA_TWO) * grad * grad
    first_hat = first_new / (1.0 - BETA_ONE**STEP)
    second_hat = second_new / (1.0 - BETA_TWO**STEP)
    param_new = param - rate * (first_hat / (jnp.sqrt(second_hat) + ADAM_EPS) + DECAY * param)
    return (param_new, first_new, second_new)


AXES = ("z1", "z0", "x", "y", "c", "r")


def on_device(
    layer_input, out_grad, matrices, mat_first, mat_second, mat_ema, gains, gain_first, gain_second,
    rel_bias, bias_first, bias_second, bucket_len, item_count, bucket_table,
):
    shards = jnp.swapaxes(matrices, 1, 2).astype(BF16)
    gathered = [lax.all_gather(shards[i], AXES, axis=0, tiled=True) for i in range(3)]
    qkv_weight = gathered[0][: 3 * D]
    out_weight = gathered[0][3 * D :]

    flipped = jnp.concatenate([bucket_table[::-1], jnp.full((1,), -1, jnp.int32)])
    onehot = (flipped[None, :] == jnp.arange(BUCKETS, dtype=jnp.int32)[:, None]).astype(F32)
    table = jnp.dot(rel_bias.T, onehot, precision=lax.Precision.HIGHEST).reshape(PAIRS, 2, SPAN)

    gain_one = gains[0:1]
    gain_two = gains[1:2]
    normed, packed = qkv_call(layer_input, gain_one, qkv_weight)
    mixed, lse = attend_call(bucket_len, item_count, packed, table)
    middle, second = middle_call(layer_input, mixed, gain_two, out_weight)
    ffn, back, grad_up, grad_down = feed_call(second, out_grad, gathered[1], gathered[2])
    dmiddle, dmixed, dgain_two, grad_out = middle_back_call(
        back, middle, out_grad, mixed, gain_two, out_weight
    )
    dq, dk, dv, dlines = attend_back_call(bucket_len, item_count, packed, dmixed, lse, table)
    grad_qkv = qkv_grad_call(dq, dk, dv, normed)
    input_grad, dgain_one = input_back_call(dq, dk, dv, layer_input, dmiddle, gain_one, qkv_weight)
    layer_output = (middle + ffn).astype(BF16)

    def scatter(value):
        return lax.psum_scatter(value, AXES, scatter_dimension=0, tiled=True)

    summed = [scatter(jnp.concatenate([grad_qkv, grad_out])), scatter(grad_up), scatter(grad_down)]
    mat_grad = jnp.swapaxes(jnp.stack(summed), 1, 2)
    bias_local = jnp.dot(onehot, dlines.reshape(HEADS, SPAN).T, precision=lax.Precision.HIGHEST)
    gain_local = jnp.concatenate([dgain_one, dgain_two])
    gain_grad, bias_grad = lax.psum((gain_local, bias_local), AXES)
    mat_new, mat_first_new, mat_second_new = adam_update(
        matrices, mat_grad, mat_first, mat_second, RATE
    )
    mat_ema_new = EMA_KEEP * mat_ema + (1.0 - EMA_KEEP) * mat_new
    gain_new, gain_first_new, gain_second_new = adam_update(
        gains, gain_grad, gain_first, gain_second, RATE_SMALL
    )
    bias_new, bias_first_new, bias_second_new = adam_update(
        rel_bias, bias_grad, bias_first, bias_second, RATE_SMALL
    )
    return (
        layer_output, input_grad, mat_grad, mat_new, mat_first_new, mat_second_new, mat_ema_new,
        gain_grad, gain_new, gain_first_new, gain_second_new,
        bias_grad, bias_new, bias_first_new, bias_second_new,
    )


def solution(mesh):
    devices = mesh.devices.size
    fine = Mesh(mesh.devices.reshape(2, 2, 2, 2, 2, devices // 32), AXES)
    rows = P(AXES, None)
    columns = P(None, None, AXES)
    return jax.shard_map(
        on_device,
        mesh=fine,
        in_specs=(rows, rows) + (columns,) * 4 + (P(),) * 6 + (P(AXES), P(AXES), P()),
        out_specs=(rows, rows) + (columns,) * 5 + (P(),) * 8,
        check_vma=False,
    )
```

time: 3100 us -> 689 us (0.22)
  local copies, waits for them, and re-layouts: 2370 us -> 14.5 us
  matrix products: 194 us -> 1 us
  Pallas kernels: 0 us -> 156 us
  waiting for transfers between devices: 329 us -> 442 us
  other arithmetic: 85.1 us -> 18.8 us
  loops' own time: 32.1 us -> 0 us
    gather x1 -> x0, local copies, waits for them, and re-layouts: 2130 us -> none  [bucket_onehot(): chosen = jnp.take(bucket_table, offsets)]
    reduce_scatter x0 -> x3, waiting for transfers between devices: none -> 295 us  [scatter(): return lax.psum_scatter(value, AXES, scatter_dimension=0, tiled=True)]
    dot_general x70 -> x2, matrix products: 194 us -> 1 us  [the longest x1 0.86 us: on_device(): jnp.dot(rel_bias.T, onehot, precision=lax.Precision.HIGHEST)]
    unnamed x3 -> x6, waiting for transfers between devices: 167 us -> 1.96 us
    all_to_all x4 -> x0, waiting for transfers between devices: 161 us -> none  [the longest x1 69.7 us: on_device(): lax.all_to_all(grad_blocks.reshape(-1, 3, heads_here * HD), 'head', split...]
    pallas_call x0 -> x8, Pallas kernels: none -> 156 us  [the longest x1 49.5 us: feed_call(): pl.pallas_call(feed_kernel, grid=(units // chunk,), in_specs=[whole((toke...]
    all_gather x1 -> x3, waiting for transfers between devices: 0.02 us -> 145 us  [on_device(): lax.all_gather(shards[i], AXES, axis=0, tiled=True)]
    unnamed x104 -> x26, local copies, waits for them, and re-layouts: 98.7 us -> 1.67 us
  transfers between devices with their start and end apart: 6 -> 6, of which waited for: 5 -> 6; matrix products, arithmetic and copies ran while one was open for 72% -> 4% of each run, Pallas kernels for 0% -> 15%
where the time goes in v1:
time: 689 us; the launch traced here: 688 us
  waiting for transfers between devices  442 us (64%)
  Pallas kernels  156 us (23%)
  blocking collectives  40.3 us (6%)
  other arithmetic  18.8 us (3%)
  between operations  14.9 us (2%)
  local copies, waits for them, and re-layouts  14.5 us (2%)
    reduce_scatter x3, waiting for transfers between devices, scatter(): return lax.psum_scatter(value, AXES, scatter_dimension=0, tiled=True)  295 us
    all_gather x3, waiting for transfers between devices, on_device(): lax.all_gather(shards[i], AXES, axis=0, tiled=True)  145 us
    pallas_call x1, Pallas kernels, feed_call(): pl.pallas_call(feed_kernel, grid=(units // chunk,), in_specs=[whole((toke...  49.5 us
    psum x1, blocking collectives, on_device(): gain_grad, bias_grad = lax.psum((gain_local, bias_local), AXES)  40.3 us
    pallas_call x1, Pallas kernels, attend_back_call(): pl.pallas_call(attend_back_kernel, grid_spec=pltpu.PrefetchScalarGridSpec...  36.2 us
    pallas_call x1, Pallas kernels, attend_call(): pl.pallas_call(attend_kernel, grid_spec=pltpu.PrefetchScalarGridSpec(num_...  25.8 us
  transfers between devices with their start and end apart: 6, of which 6 were waited for; matrix products, arithmetic and copies ran while one was open for 4% of the time, Pallas kernels for 15%

profile of v1, /device:TPU:0, one launch (start us, length us, event | category | flops | bytes accessed | tf_op | source)
XLA Modules:
  0.0 687.6 jit_solution(10099902647049317893)
XLA Ops:
  7.2 0.0 all-gather.7.cloned.1.call-start
  7.2 1.2 convert_bitcast_fusion
  8.4 0.8 fusion.9
  9.2 0.0 all-gather.7.cloned.1.call-update
  9.2 0.0 all-gather.11.cloned.1.call-start
  9.3 0.7 all-gather.11.cloned.1.call-update
  10.0 0.0 all-gather.9.cloned.1.call-start
  10.0 0.7 all-gather.9.cloned.1.call-update
  10.7 0.0 reduce-scatter.6.cloned.1.call-start
  10.8 1.2 dynamic-slice.2
  12.7 1.2 dynamic-slice.3.len_ref
  13.9 1.2 dynamic-slice.7.count_ref
  15.2 0.8 reverse
  15.9 0.1 slice.37
  16.0 0.1 pad_add_fusion
  16.1 0.9 convolution_bitcast_fusion
  16.9 0.7 reshape.43.table_ref
  17.6 1.4 fusion.10
  18.9 58.9 %all-gather.7.cloned.1.call-done = bf16[1,3072,768]{2,1,0:T(8,128)(2,1)} async-done(((bf16[1,96,768]{2,1,0:T(8,128)(2,1)}), bf16[1,3072,768]{2,1,0:T(8,128)(2,1)}) %all-gather.7.cloned.1.call-update) | async-done | bytes 4718608 | tf_op jit(solution)/shard_map/all_gather | solution.py:517
  77.8 2.4 slice_bitcast_fusion.1.weight_ref
  80.2 4.0 slice_bitcast_fusion.weight_ref
  84.2 8.1 %norm_qkv.1 = (bf16[1024,768]{1,0:T(8,128)(2,1)}, bf16[1024,2304]{1,0:T(8,128)(2,1)}) custom-call(bf16[1024,768]{1,0:T(8,128)(2,1)} %x_ref.5, f32[1,768]{1,0:T(1,128)} %get-tuple-element.72.gain_ref, bf16[2304,768]{1,0:T(8,128)(2,1)} %slice_bitcast_fusion.weight_ref), custom_call_target="tpu_custom_call" | custom-call | flops 3623878656 | bytes 16000000 | tf_op jit(solution)/shard_map/norm_qkv/pallas_call | solution.py:74
  92.2 25.8 %attend.1 = (bf16[1024,768]{1,0:T(8,128)(2,1)}, f32[1024,768]{1,0:T(8,128)}) custom-call(s32[2]{0:T(128)} %dynamic-slice.3.len_ref, s32[2]{0:T(128)} %dynamic-slice.7.count_ref, bf16[1024,2304]{1,0:T(8,128)(2,1)} %get-tuple-element.35.q_ref.k_ref.v_ref, bf16[1024,2304]{1,0:T(8,128)(2,1)} %get-tuple-element.35.q_ref.k_ref.v_ref, ...), custom_call_target="tpu_custom_call" | custom-call | flops 12000000000 | bytes 10000000 | tf_op jit(solution)/shard_map/attend/pallas_call | solution.py:178
  118.0 5.9 middle.1
  123.9 19.9 %all-gather.11.cloned.1.call-done = bf16[1,3072,768]{2,1,0:T(8,128)(2,1)} async-done(((bf16[1,96,768]{2,1,0:T(8,128)(2,1)}), bf16[1,3072,768]{2,1,0:T(8,128)(2,1)}) %all-gather.11.cloned.1.call-update) | async-done | bytes 4718608 | tf_op jit(solution)/shard_map/all_gather | solution.py:517
  143.8 65.9 %all-gather.9.cloned.1.call-done = bf16[1,3072,768]{2,1,0:T(8,128)(2,1)} async-done(((bf16[1,96,768]{2,1,0:T(8,128)(2,1)}), bf16[1,3072,768]{2,1,0:T(8,128)(2,1)}) %all-gather.9.cloned.1.call-update) | async-done | bytes 4718608 | tf_op jit(solution)/shard_map/all_gather | solution.py:517
  209.8 49.5 %feed.1 = (f32[1024,768]{1,0:T(8,128)}, f32[1024,768]{1,0:T(8,128)}, f32[3072,768]{1,0:T(8,128)}, f32[3072,768]{1,0:T(8,128)}) custom-call(bf16[1024,768]{1,0:T(8,128)(2,1)} %get-tuple-element.38.second_ref, bf16[1024,768]{1,0:T(8,128)(2,1)} %grad_ref.3, bf16[3072,768]{1,0:T(8,128)(2,1)} %bitcast.25, bf16[3072,768]{1,0:T(8,128)(2,1)} %bitcast.24), custom_call_target="tpu_custom_call" | custom-call | flops 28991029248 | bytes 40000000 | tf_op jit(solution)/shard_map/feed/pallas_call | solution.py:377
  259.2 0.0 reduce-scatter.6.cloned.1.call-update
  259.3 0.0 reduce-scatter.8.cloned.1.call-start
  259.3 0.5 reduce-scatter.8.cloned.1.call-update
  259.9 0.2 reduce-scatter.4.cloned.1.call-start
  260.1 10.3 %middle_back.1 = (f32[1024,768]{1,0:T(8,128)}, bf16[1024,768]{1,0:T(8,128)(2,1)}, f32[1,768]{1,0:T(1,128)}, f32[768,768]{1,0:T(8,128)}) custom-call(f32[1024,768]{1,0:T(8,128)} %get-tuple-element.40.part_ref, f32[1024,768]{1,0:T(8,128)} %get-tuple-element.37.middle_ref, bf16[1024,768]{1,0:T(8,128)(2,1)} %grad_ref.3, ...), custom_call_target="tpu_custom_call" | custom-call | flops 2415919104 | bytes 18000000 | tf_op jit(solution)/shard_map/middle_back/pallas_call | solution.py:420
  270.4 36.2 %attend_back.1 = (bf16[1024,768]{1,0:T(8,128)(2,1)}, bf16[1024,768]{1,0:T(8,128)(2,1)}, bf16[1024,768]{1,0:T(8,128)(2,1)}, f32[6,2,1024]{2,1,0:T(2,128)}) custom-call(s32[2]{0:T(128)} %dynamic-slice.3.len_ref, s32[2]{0:T(128)} %dynamic-slice.7.count_ref, bf16[1024,2304]{1,0:T(8,128)(2,1)} %get-tuple-element.35.q_ref.k_ref.v_ref, ...), custom_call_target="tpu_custom_call" | custom-call | flops 30000001024 | bytes 16000000 | tf_op jit(solution)/shard_map/attend_back/pallas_call | solution.py:288
  306.6 9.9 %qkv_grad.1 = f32[2304,768]{1,0:T(8,128)} custom-call(bf16[1024,768]{1,0:T(8,128)(2,1)} %get-tuple-element.43.dq_ref, bf16[1024,768]{1,0:T(8,128)(2,1)} %get-tuple-element.44.dk_ref, bf16[1024,768]{1,0:T(8,128)(2,1)} %get-tuple-element.45.dv_ref, bf16[1024,768]{1,0:T(8,128)(2,1)} %get-tuple-element.48.normed_ref), custom_call_target="tpu_custom_call" | custom-call | flops 3623878656 | bytes 16000000 | tf_op jit(solution)/shard_map/qkv_grad/pallas_call | solution.py:453
  316.4 7.3 %pad_maximum_fusion = f32[3072,768]{1,0:T(8,128)} fusion(f32[768,768]{1,0:T(8,128)S(1)} %copy-done.1, f32[2304,768]{1,0:T(8,128)} %qkv_grad.1), kind=kLoop, calls=%fused_computation | loop fusion | flops 2359296 | bytes 18874368 | tf_op jit(solution)/shard_map/concatenate | solution.py:542
  323.8 0.0 reduce-scatter.4.cloned.1.call-update
  323.8 0.8 copy-done.2
  324.7 10.1 %input_back.1 = (f32[1024,768]{1,0:T(8,128)}, f32[1,768]{1,0:T(1,128)}) custom-call(bf16[1024,768]{1,0:T(8,128)(2,1)} %get-tuple-element.43.dq_ref, bf16[1024,768]{1,0:T(8,128)(2,1)} %get-tuple-element.44.dk_ref, bf16[1024,768]{1,0:T(8,128)(2,1)} %get-tuple-element.45.dv_ref, bf16[1024,768]{1,0:T(8,128)(2,1)} %x_ref.5, ...), custom_call_target="tpu_custom_call" | custom-call | flops 3623878656 | bytes 18000000 | tf_op jit(solution)/shard_map/input_back/pallas_call | solution.py:488
  334.8 0.7 pad_maximum_fusion.1
  335.5 0.1 fusion.1
  335.7 40.3 %all-reduce = (f32[2,768]{1,0:T(2,128)S(1)}, f32[32,12]{0,1:T(8,128)S(1)}) all-reduce(f32[2,768]{1,0:T(2,128)S(1)} %pad_maximum_fusion.1, f32[32,12]{0,1:T(8,128)S(1)} %fusion.1), channel_id=1, replica_groups=mesh['z1'=2,'z0'=2,'x'=2,'y'=2,'c'=2,'r'=1] {'z1','z0','x','y','c','r'}, use_global_device_ids=true, to_apply=%region_3.0 | all-reduce | flops 1920 | bytes 15360 | tf_op jit(solution)/shard_map/psum | solution.py:546
  375.9 0.6 multiply_subtract_fusion.2
  376.6 0.6 multiply_subtract_fusion.1
  377.2 3.3 add_convert_fusion
  380.5 13.6 %reduce-scatter.6.cloned.1.call-done = f32[96,768]{1,0:T(8,128)} async-done(((f32[3072,768]{1,0:T(8,128)}), f32[96,768]{1,0:T(8,128)}) %reduce-scatter.6.cloned.1.call-update) | async-done | bytes 294928 | tf_op jit(solution)/shard_map/reduce_scatter | solution.py:540
  394.1 141.4 %reduce-scatter.8.cloned.1.call-done = f32[96,768]{1,0:T(8,128)} async-done(((f32[3072,768]{1,0:T(8,128)}), f32[96,768]{1,0:T(8,128)}) %reduce-scatter.8.cloned.1.call-update) | async-done | bytes 294928 | tf_op jit(solution)/shard_map/reduce_scatter | solution.py:540
  535.5 140.3 %reduce-scatter.4.cloned.1.call-done = f32[96,768]{1,0:T(8,128)} async-done(((f32[3072,768]{1,0:T(8,128)}), f32[96,768]{1,0:T(8,128)}) %reduce-scatter.4.cloned.1.call-update) | async-done | bytes 294928 | tf_op jit(solution)/shard_map/reduce_scatter | solution.py:540
  675.8 4.9 multiply_add_fusion
  (24 shorter events, 0.1 us)
Async XLA Ops:
  7.2 70.6 %all-gather.7.cloned.1.call-start = ((), (), s32[]{:S(2)}) async-start(), calls=%async_computation.6 | async-start | bytes 4866048 | tf_op jit(solution)/shard_map/all_gather | solution.py:517
  9.2 134.6 %all-gather.11.cloned.1.call-start = ((), (), s32[]{:S(2)}) async-start(), calls=%async_computation.8 | async-start | bytes 4866048 | tf_op jit(solution)/shard_map/all_gather | solution.py:517
  10.0 199.8 %all-gather.9.cloned.1.call-start = ((), (), s32[]{:S(2)}) async-start(), calls=%async_computation.7 | async-start | bytes 4866048 | tf_op jit(solution)/shard_map/all_gather | solution.py:517
  10.7 383.4 %reduce-scatter.6.cloned.1.call-start = ((), (), s32[]{:S(2)}) async-start(), calls=%async_computation.4 | async-start | bytes 9732096 | tf_op jit(solution)/shard_map/reduce_scatter | solution.py:540
  259.3 276.2 %reduce-scatter.8.cloned.1.call-start = ((), (), s32[]{:S(2)}) async-start(), calls=%async_computation.5 | async-start | bytes 9732096 | tf_op jit(solution)/shard_map/reduce_scatter | solution.py:540
  259.9 416.0 %reduce-scatter.4.cloned.1.call-start = ((), (), s32[]{:S(2)}) async-start(), calls=%async_computation.3 | async-start | bytes 9732096 | tf_op jit(solution)/shard_map/reduce_scatter | solution.py:540
  306.5 9.9 %copy-start.1 = (f32[768,768]{1,0:T(8,128)S(1)}, f32[768,768]{1,0:T(8,128)}, u32[]{:S(2)}) copy-start(f32[768,768]{1,0:T(8,128)} %get-tuple-element.49) | copy-start | bytes 7077892
  323.8 0.8 copy-start.2
  324.6 10.2 %copy-start.11 = (f32[1,768]{1,0:T(1,128)S(1)}, f32[1,768]{1,0:T(1,128)}, u32[]{:S(2)}) copy-start(f32[1,768]{1,0:T(1,128)} %get-tuple-element.53) | copy-start | bytes 9220
  324.6 51.3 %copy-start.4 = (f32[2,768]{1,0:T(2,128)S(1)}, f32[2,768]{1,0:T(2,128)}, u32[]{:S(2)}) copy-start(f32[2,768]{1,0:T(2,128)} %param.21) | copy-start | bytes 18436
  324.6 51.3 %copy-start.8 = (f32[2,768]{1,0:T(2,128)S(1)}, f32[2,768]{1,0:T(2,128)}, u32[]{:S(2)}) copy-start(f32[2,768]{1,0:T(2,128)} %param.22) | copy-start | bytes 18436
  324.6 51.3 %copy-start.9 = (f32[2,768]{1,0:T(2,128)S(1)}, f32[2,768]{1,0:T(2,128)}, u32[]{:S(2)}) copy-start(f32[2,768]{1,0:T(2,128)} %param.23) | copy-start | bytes 18436
  324.6 51.9 %copy-start.3 = (f32[32,12]{0,1:T(8,128)S(1)}, f32[32,12]{0,1:T(8,128)}, u32[]{:S(2)}) copy-start(f32[32,12]{0,1:T(8,128)} %param.24) | copy-start | bytes 4612
  324.7 51.9 %copy-start.5 = (f32[32,12]{0,1:T(8,128)S(1)}, f32[32,12]{0,1:T(8,128)}, u32[]{:S(2)}) copy-start(f32[32,12]{0,1:T(8,128)} %param.25) | copy-start | bytes 4612
  324.7 51.9 %copy-start.6 = (f32[32,12]{0,1:T(8,128)S(1)}, f32[32,12]{0,1:T(8,128)}, u32[]{:S(2)}) copy-start(f32[32,12]{0,1:T(8,128)} %param.26) | copy-start | bytes 4612
  324.7 52.5 %copy-start = (f32[1024,768]{1,0:T(8,128)S(1)}, f32[1024,768]{1,0:T(8,128)}, u32[]{:S(2)}) copy-start(f32[1024,768]{1,0:T(8,128)} %get-tuple-element.37.middle_ref) | copy-start | bytes 9437188
  375.9 4.6 copy-start.7
  375.9 4.6 copy-start.10
Sparse Core Ops, SparseCore 0:
  11.5 66.2 all-gather.6
  81.3 62.5 all-gather.10
  147.3 62.3 all-gather.8
  259.4 134.6 reduce-scatter.5
  400.8 134.5 reduce-scatter.7
  541.2 134.5 reduce-scatter.3

commit v2 on v1

v2 whole, which is shorter than its diff:
```python
import functools

import jax
import jax.numpy as jnp
from jax import lax
from jax.experimental import pallas as pl
from jax.experimental.pallas import tpu as pltpu
from jax.sharding import Mesh, PartitionSpec as P

D = 768
FF = 3072
HEADS = 12
HD = 64
BUCKETS = 32
ROW = 512
STEP = 10
PAIRS = HEADS // 2
WIDE = 2 * HD
SUB = 128
QB = 256
SPAN = 1024
TOEP = 896

EPS = 1e-06
RATE = 0.05
RATE_SMALL = 0.5
BETA_ONE = 0.9
BETA_TWO = 0.999
ADAM_EPS = 1e-08
DECAY = 0.1
EMA_KEEP = 0.75

F32 = jnp.float32
BF16 = jnp.bfloat16
VMEM_LIMIT = 56 * 1024 * 1024
TILE = 256
SHARD = 96
HALF = 48
PIECES = 8
AHEAD = 3
FIRST = 4

NN = (((1,), (0,)), ((), ()))
NT = (((1,), (1,)), ((), ()))
TN = (((0,), (0,)), ((), ()))


def dot(left, right, dims):
    return lax.dot_general(left, right, dims, preferred_element_type=F32)


def params(**more):
    return pltpu.CompilerParams(vmem_limit_bytes=VMEM_LIMIT, **more)


def cost(flops, moved, special=0):
    return pl.CostEstimate(flops=int(flops), bytes_accessed=int(moved), transcendentals=int(special))


def whole(shape):
    return pl.BlockSpec(shape, lambda *_: (0,) * len(shape))


def tiles(rows, columns):
    return pl.BlockSpec((rows, columns), lambda i, *_: (i, 0))


def piece_block():
    return pl.BlockSpec((4 * HALF, D), lambda i: (0, 0), pipeline_mode=pl.Buffered(1))


def fill_toeplitz(table_ref, toep):
    for h in range(2):
        line = jnp.broadcast_to(table_ref[0, h : h + 1, :], (SUB, SPAN))
        rolled = pltpu.roll(line, SPAN - (SUB - 1), 1, stride=1, stride_axis=0)
        toep[h] = rolled[:, :TOEP]


def head_masks():
    lane = lax.broadcasted_iota(jnp.int32, (1, WIDE), 1)
    return [(lane < HD).astype(BF16), (lane >= HD).astype(BF16)]


def bias_block(toep, h, first, rows, span):
    parts = []
    for t in range(rows // SUB):
        left = ROW - SUB - first - t * SUB
        parts.append(toep[h, :, left : left + span])
    return parts[0] if len(parts) == 1 else jnp.concatenate(parts, axis=0)


def blocks_of(span):
    rows = min(span, QB)
    return [(start, first, rows) for start in range(0, ROW, span) for first in range(0, span, rows)]


def live_rows(live, first, rows):
    return first + lax.broadcasted_iota(jnp.int32, (rows, 1), 0) < live


def attend(pairs, offset, rows, len_ref, count_ref, packed, table_ref, toep, mixed_ref, lse_ref):
    masks = head_masks()
    lane = lax.broadcasted_iota(jnp.int32, (1, WIDE), 1)

    @pl.loop(0, pairs)
    def _(pair):
        fill_toeplitz(table_ref.at[pl.ds(pair + offset, 1)], toep)

        @pl.loop(0, rows)
        def _(row):
            length = len_ref[row]
            live = length * count_ref[row]
            at = pl.ds(pl.multiple_of(row * ROW, ROW), ROW)
            cols = columns_of(pair, (0, packed.shape[1] // 3 // WIDE, packed.shape[1] // 3 * 2 // WIDE))
            to = columns_of(pair, (offset,))[0]

            def body(span):
                q_all, k_all, v_all = (packed[at, c] for c in cols)
                stats_all = lse_ref[at, :]
                spots = blocks_of(span)
                keys = [k_all * m for m in masks]
                vals = [v_all * m for m in masks]
                both = [(spot, h) for spot in spots for h in range(2)]
                scores = [
                    dot(q_all[start + first : start + first + rows], keys[h][start : start + span], NT)
                    + bias_block(toep, h, first, rows, span)
                    for (start, first, rows), h in both
                ]
                tops = [jnp.max(s, axis=-1, keepdims=True) for s in scores]
                exps = [jnp.exp(s - top) for s, top in zip(scores, tops)]
                totals = [jnp.sum(e, axis=-1, keepdims=True) for e in exps]
                probs = [(e * (1.0 / total)).astype(BF16) for e, total in zip(exps, totals)]
                outs_h = [
                    dot(p, vals[h][start : start + span], NN) for p, ((start, first, rows), h) in zip(probs, both)
                ]
                mixed_parts, stats_parts = [], []
                for i, (start, first, rows) in enumerate(spots):
                    mixed = outs_h[2 * i] + outs_h[2 * i + 1]
                    stats = stats_all[start + first : start + first + rows]
                    for h in range(2):
                        head = (pair + offset) * 2 + h
                        stats = jnp.where(lane == head, tops[2 * i + h] + jnp.log(totals[2 * i + h]), stats)
                    if span < ROW:
                        mixed = jnp.where(live_rows(live, start + first, rows), mixed, 0.0)
                    mixed_parts.append(mixed.astype(BF16))
                    stats_parts.append(stats)
                mixed_ref[at, to] = jnp.concatenate(mixed_parts, axis=0)
                lse_ref[at, :] = jnp.concatenate(stats_parts, axis=0)

            for span in (ROW, ROW // 2, ROW // 4):
                pl.when(length == span)(functools.partial(body, span))


def first_forward_kernel(me_ref, len_ref, count_ref, *refs):
    pieces = refs[:PIECES]
    (
        x_ref, gain_ref, table_ref, normed_out, packed_out, weight_out, lse_ref, mixed_ref,
        weight, normed, packed, toep, in_sem, out_sem,
    ) = refs[PIECES:]
    copies = []
    for i, ref in enumerate(pieces):
        core, half, far = i // 4, i // 2 % 2, i % 2
        for j in range(8):
            near, z = j // 4, j % 4
            plane = near * 2 + far if half == 0 else far * 2 + near
            owner = me_ref[0] ^ (z * 8 + plane * 2 + core)
            row = pl.multiple_of(owner * SHARD + half * HALF, 16)
            copies.append(
                pltpu.make_async_copy(ref.at[pl.ds(j * HALF, HALF)], weight.at[pl.ds(row, HALF)], in_sem)
            )
    for copy in copies:
        copy.start()

    tokens = x_ref.shape[0]

    @pl.loop(0, tokens // TILE)
    def _(tile):
        at = pl.ds(pl.multiple_of(tile * TILE, TILE), TILE)
        x = x_ref[at, :].astype(F32)
        scale = lax.rsqrt(jnp.mean(x * x, axis=-1, keepdims=True) + EPS)
        normed[at, :] = (x * scale * gain_ref[0:1, :]).astype(BF16)

    for copy in copies:
        copy.wait()
    outs = [
        pltpu.make_async_copy(weight, weight_out, out_sem.at[0]),
        pltpu.make_async_copy(normed, normed_out, out_sem.at[1]),
        pltpu.make_async_copy(packed, packed_out, out_sem.at[2]),
    ]
    outs[0].start()
    outs[1].start()

    @pl.loop(0, tokens // TILE)
    def _(tile):
        at = pl.ds(pl.multiple_of(tile * TILE, TILE), TILE)
        for part in range(3):
            cols = slice(part * D, (part + 1) * D)
            packed[at, cols] = dot(normed[at, :], weight[cols, :], NT).astype(BF16)

    outs[2].start()
    lse_ref[...] = jnp.zeros_like(lse_ref)
    attend(AHEAD, 0, tokens // ROW, len_ref, count_ref, packed, table_ref, toep, mixed_ref, lse_ref)
    for copy in outs:
        copy.wait()


def first_forward_call(me, lengths, counts, pieces, x, gains, table):
    tokens = x.shape[0]
    anywhere = pl.BlockSpec(memory_space=pl.ANY)
    inside = pl.BlockSpec(memory_space=pltpu.VMEM)
    return pl.pallas_call(
        first_forward_kernel,
        grid_spec=pltpu.PrefetchScalarGridSpec(
            num_scalar_prefetch=3,
            grid=(),
            in_specs=[anywhere] * PIECES + [inside] * 3,
            out_specs=[anywhere] * 3 + [inside] * 2,
            scratch_shapes=[
                pltpu.VMEM((4 * D, D), BF16),
                pltpu.VMEM((tokens, D), BF16),
                pltpu.VMEM((tokens, 3 * D), BF16),
                pltpu.VMEM((2, SUB, TOEP), F32),
                pltpu.SemaphoreType.DMA,
                pltpu.SemaphoreType.DMA((3,)),
            ],
        ),
        out_shape=[
            jax.ShapeDtypeStruct((tokens, D), BF16),
            jax.ShapeDtypeStruct((tokens, 3 * D), BF16),
            jax.ShapeDtypeStruct((4 * D, D), BF16),
            jax.ShapeDtypeStruct((tokens, WIDE), F32),
            jax.ShapeDtypeStruct((tokens, AHEAD * WIDE), BF16),
        ],
        compiler_params=params(),
        cost_estimate=cost(12e9, 30e6, 4e6),
        name="first_forward",
    )(me, lengths, counts, *pieces, x, gains, table)


def last_forward_kernel(
    len_ref, count_ref, x_ref, gain_ref, table_ref, first_ref, stats_ref, weight_in, packed_in,
    lse_ref, mixed_ref, middle_out, second_out,
    weight, packed, middle_s, second_s, toep, in_sems, out_sems,
):
    tokens = x_ref.shape[0]
    start = AHEAD * WIDE
    width = D - start
    copies = [pltpu.make_async_copy(weight_in.at[pl.ds(3 * D, D)], weight, in_sems.at[0])]
    for part in range(3):
        copies.append(
            pltpu.make_async_copy(
                packed_in.at[:, pl.ds(part * D + start, width)], packed.at[:, pl.ds(part * width, width)], in_sems.at[1 + part]
            )
        )
    for copy in copies:
        copy.start()
    lse_ref[...] = stats_ref[...]
    mixed_ref[:, :start] = first_ref[...]
    for copy in copies[1:]:
        copy.wait()
    attend(PAIRS - AHEAD, AHEAD, tokens // ROW, len_ref, count_ref, packed, table_ref, toep, mixed_ref, lse_ref)
    copies[0].wait()
    outs = []
    for tile in range(tokens // TILE):
        at = pl.ds(tile * TILE, TILE)
        middle = x_ref[at, :].astype(F32) + dot(mixed_ref[at, :], weight[...], NT)
        middle_s[at, :] = middle
        scale = lax.rsqrt(jnp.mean(middle * middle, axis=-1, keepdims=True) + EPS)
        second_s[at, :] = (middle * scale * gain_ref[1:2, :]).astype(BF16)
        for i, (src, dst) in enumerate(((middle_s, middle_out), (second_s, second_out))):
            copy = pltpu.make_async_copy(src.at[at], dst.at[at], out_sems.at[2 * tile + i])
            copy.start()
            outs.append(copy)
    for copy in outs:
        copy.wait()


def last_forward_call(lengths, counts, x, gains, table, first, stats, weight, packed):
    tokens = x.shape[0]
    anywhere = pl.BlockSpec(memory_space=pl.ANY)
    inside = pl.BlockSpec(memory_space=pltpu.VMEM)
    flat = jax.ShapeDtypeStruct((tokens, D), BF16)
    return pl.pallas_call(
        last_forward_kernel,
        grid_spec=pltpu.PrefetchScalarGridSpec(
            num_scalar_prefetch=2,
            grid=(),
            in_specs=[inside] * 5 + [anywhere] * 2,
            out_specs=[inside] * 2 + [anywhere] * 2,
            scratch_shapes=[
                pltpu.VMEM((D, D), BF16),
                pltpu.VMEM((tokens, 3 * (PAIRS - AHEAD) * WIDE), BF16),
                pltpu.VMEM((tokens, D), F32),
                pltpu.VMEM((tokens, D), BF16),
                pltpu.VMEM((2, SUB, TOEP), F32),
                pltpu.SemaphoreType.DMA((4,)),
                pltpu.SemaphoreType.DMA((2 * tokens // TILE,)),
            ],
        ),
        out_shape=[
            jax.ShapeDtypeStruct((tokens, WIDE), F32),
            flat,
            jax.ShapeDtypeStruct((tokens, D), F32),
            flat,
        ],
        compiler_params=params(),
        cost_estimate=cost(8e9, 20e6, 4e6),
        name="last_forward",
    )(lengths, counts, x, gains, table, first, stats, weight, packed)


def fold_diagonals(grid):
    height = SUB
    total = jnp.concatenate([grid, jnp.zeros((SUB, SPAN - TOEP), F32)], axis=1)
    while height > 8:
        height //= 2
        total = pltpu.roll(total[:height], height, 1) + total[height:]
    line = total[7:8]
    for r in range(7):
        line = line + pltpu.roll(total, 7 - r, 1)[r : r + 1]
    return line


def attend_back(
    pairs, offset, me_rows, len_ref, count_ref, cols_of, packed, dmixed, lse_ref, table_ref, toep, diag, out_ref, dbias_ref
):
    masks = head_masks()
    lane = lax.broadcasted_iota(jnp.int32, (1, WIDE), 1)

    @pl.loop(0, pairs)
    def _(pair):
        fill_toeplitz(table_ref.at[pl.ds(pair + offset, 1)], toep)
        diag[...] = jnp.zeros_like(diag)

        @pl.loop(0, me_rows)
        def _(row):
            length = len_ref[row]
            live = length * count_ref[row]
            at = pl.ds(pl.multiple_of(row * ROW, ROW), ROW)
            cols = cols_of(pair)

            def body(span):
                q_all, k_all, v_all = (packed[at, c] for c in cols[:3])
                do_all = dmixed[at, cols[3]]
                if span < ROW:
                    do_all = jnp.where(live_rows(live, 0, ROW), do_all.astype(F32), 0.0).astype(BF16)
                stats = lse_ref[at, :]
                spots = blocks_of(span)
                queries, keys, vals, dos = ([a * m for m in masks] for a in (q_all, k_all, v_all, do_all))
                lses = [
                    jnp.sum(jnp.where(lane == (pair + offset) * 2 + h, stats, 0.0), axis=-1, keepdims=True) for h in range(2)
                ]
                both = [(spot, h) for spot in spots for h in range(2)]

                def rows_of(value, spot):
                    return value[spot[0] + spot[1] : spot[0] + spot[1] + spot[2]]

                def keys_of(value, spot):
                    return value[spot[0] : spot[0] + span]

                scores = [
                    dot(rows_of(q_all, spot), keys_of(keys[h], spot), NT) + bias_block(toep, h, spot[1], spot[2], span)
                    for spot, h in both
                ]
                dps = [dot(rows_of(do_all, spot), keys_of(vals[h], spot), NT) for spot, h in both]
                probs = [jnp.exp(s - rows_of(lses[h], spot)) for s, (spot, h) in zip(scores, both)]
                parts = [p * dp for p, dp in zip(probs, dps)]
                sums = [jnp.sum(t, axis=-1, keepdims=True) for t in parts]
                dss = [t - p * total for t, p, total in zip(parts, probs, sums)]
                for ds, (spot, h) in zip(dss, both):
                    for sub in range(spot[2] // SUB):
                        left = ROW - SUB - spot[1] - sub * SUB
                        diag[h, :, left : left + span] += ds[sub * SUB : (sub + 1) * SUB]
                lows = [ds.astype(BF16) for ds in dss]
                plows = [p.astype(BF16) for p in probs]
                dqs = [dot(low, keys_of(keys[h], spot), NN) for low, (spot, h) in zip(lows, both)]
                dks = [dot(low, rows_of(queries[h], spot), TN) for low, (spot, h) in zip(lows, both)]
                dvs = [dot(low, rows_of(dos[h], spot), TN) for low, (spot, h) in zip(plows, both)]
                dq = jnp.concatenate([dqs[2 * i] + dqs[2 * i + 1] for i in range(len(spots))], axis=0)
                each = len(both) * span // ROW
                dk, dv = (
                    jnp.concatenate([sum(d[i + 1 : i + each], d[i]) for i in range(0, len(both), each)], axis=0)
                    for d in (dks, dvs)
                )
                for part, value in enumerate((dq, dk, dv)):
                    to = pl.ds(pl.multiple_of(pair * WIDE + part * pairs * WIDE, WIDE), WIDE)
                    out_ref[at, to] = value.astype(BF16)

            for span in (ROW, ROW // 2, ROW // 4):
                pl.when(length == span)(functools.partial(body, span))

        for h in range(2):
            dbias_ref[pl.ds(pair, 1), h : h + 1, :] = fold_diagonals(diag[h]).reshape(1, 1, SPAN)


def columns_of(pair, widths):
    return [pl.ds(pl.multiple_of((pair + w) * WIDE, WIDE), WIDE) for w in widths]


def first_back_kernel(
    len_ref, count_ref, mixed_ref, gain_ref, lse_ref, table_ref,
    part_in, got_in, middle_in, grad_in, weight_in, packed_in,
    dgain_ref, out_ref, dbias_ref, dmiddle_out, dmixed_out, dweight_out,
    part_s, got_s, middle_s, grad_s, dmixed, dweight, weight, packed, lows, toep, diag, in_sems, sems, out_sems,
):
    tokens = mixed_ref.shape[0]
    count = tokens // TILE
    width = FIRST * WIDE
    first = pltpu.make_async_copy(weight_in.at[pl.ds(3 * D, D)], weight, sems.at[0])
    first.start()
    ins = []
    for tile in range(count):
        at = pl.ds(tile * TILE, TILE)
        for i, (src, dst) in enumerate(((part_in, part_s), (got_in, got_s), (middle_in, middle_s), (grad_in, grad_s))):
            copy = pltpu.make_async_copy(src.at[at], dst.at[at], in_sems.at[4 * tile + i])
            copy.start()
            ins.append(copy)
    later = []
    for part in range(3):
        copy = pltpu.make_async_copy(
            packed_in.at[:, pl.ds(part * D, width)], packed.at[:, pl.ds(part * width, width)], sems.at[1 + part]
        )
        copy.start()
        later.append(copy)
    first.wait()
    outs = []
    dgain = jnp.zeros((1, D), F32)
    for tile in range(count):
        at = pl.ds(tile * TILE, TILE)
        for copy in ins[4 * tile : 4 * tile + 4]:
            copy.wait()
        db = part_s[at, :] + got_s[at, :]
        middle = middle_s[at, :]
        scale = lax.rsqrt(jnp.mean(middle * middle, axis=-1, keepdims=True) + EPS)
        dn = db * gain_ref[1:2, :]
        inner = jnp.mean(dn * middle, axis=-1, keepdims=True)
        dmiddle = grad_s[at, :].astype(F32) + scale * dn - middle * (scale * scale * scale * inner)
        part_s[at, :] = dmiddle
        copy = pltpu.make_async_copy(part_s.at[at], dmiddle_out.at[at], out_sems.at[tile])
        copy.start()
        outs.append(copy)
        low = dmiddle.astype(BF16)
        lows[at, :] = low
        dmixed[at, :] = dot(low, weight[...], NN).astype(BF16)
        dgain += jnp.sum(db * middle * scale, axis=0, keepdims=True)
    dgain_ref[...] = dgain
    copy = pltpu.make_async_copy(dmixed, dmixed_out, out_sems.at[count])
    copy.start()
    outs.append(copy)
    dweight[...] = dot(lows[...], mixed_ref[...], TN)
    copy = pltpu.make_async_copy(dweight, dweight_out, out_sems.at[count + 1])
    copy.start()
    outs.append(copy)
    for copy in later:
        copy.wait()

    def cols_of(pair):
        return columns_of(pair, (0, FIRST, 2 * FIRST, 0))

    attend_back(
        FIRST, 0, tokens // ROW, len_ref, count_ref, cols_of, packed, dmixed, lse_ref, table_ref, toep, diag, out_ref, dbias_ref
    )
    for copy in outs:
        copy.wait()


def first_back_call(lengths, counts, part, got, middle, out_grad, mixed, gains, lse, table, weight, packed):
    tokens = part.shape[0]
    anywhere = pl.BlockSpec(memory_space=pl.ANY)
    inside = pl.BlockSpec(memory_space=pltpu.VMEM)
    width = 3 * FIRST * WIDE
    count = tokens // TILE
    return pl.pallas_call(
        first_back_kernel,
        grid_spec=pltpu.PrefetchScalarGridSpec(
            num_scalar_prefetch=2,
            grid=(),
            in_specs=[inside] * 4 + [anywhere] * 6,
            out_specs=[inside] * 3 + [anywhere] * 3,
            scratch_shapes=[pltpu.VMEM((tokens, D), F32)] * 3
            + [
                pltpu.VMEM((tokens, D), BF16),
                pltpu.VMEM((tokens, D), BF16),
                pltpu.VMEM((D, D), F32),
                pltpu.VMEM((D, D), BF16),
                pltpu.VMEM((tokens, width), BF16),
                pltpu.VMEM((tokens, D), BF16),
                pltpu.VMEM((2, SUB, TOEP), F32),
                pltpu.VMEM((2, SUB, TOEP), F32),
                pltpu.SemaphoreType.DMA((4 * count,)),
                pltpu.SemaphoreType.DMA((4,)),
                pltpu.SemaphoreType.DMA((count + 2,)),
            ],
        ),
        out_shape=[
            jax.ShapeDtypeStruct((1, D), F32),
            jax.ShapeDtypeStruct((tokens, width), BF16),
            jax.ShapeDtypeStruct((FIRST, 2, SPAN), F32),
            jax.ShapeDtypeStruct((tokens, D), F32),
            jax.ShapeDtypeStruct((tokens, D), BF16),
            jax.ShapeDtypeStruct((D, D), F32),
        ],
        compiler_params=params(),
        cost_estimate=cost(15e9, 30e6, 7e6),
        name="first_back",
    )(lengths, counts, mixed, gains, lse, table, part, got, middle, out_grad, weight, packed)


def last_back_kernel(
    me_ref, len_ref, count_ref, lse_ref, table_ref, normed_in, first_in, dout_in, packed_in, dmixed_in,
    out_ref, dbias_ref, own_out, other_out,
    packed, dmixed, normed, first, own, other, total, toep, diag, sems, out_sems,
):
    tokens = normed.shape[0]
    pairs = PAIRS - FIRST
    width = pairs * WIDE
    start = FIRST * WIDE
    copies = [pltpu.make_async_copy(dmixed_in.at[:, pl.ds(start, width)], dmixed, sems.at[0])]
    for part in range(3):
        copies.append(
            pltpu.make_async_copy(
                packed_in.at[:, pl.ds(part * D + start, width)], packed.at[:, pl.ds(part * width, width)], sems.at[1 + part]
            )
        )
    later = [
        pltpu.make_async_copy(normed_in, normed, sems.at[4]),
        pltpu.make_async_copy(first_in, first, sems.at[5]),
        pltpu.make_async_copy(dout_in, total.at[pl.ds(3 * D, D)], sems.at[6]),
    ]
    for copy in copies + later:
        copy.start()
    for copy in copies:
        copy.wait()

    def cols_of(pair):
        return columns_of(pair, (0, pairs, 2 * pairs, 0))

    attend_back(
        pairs, FIRST, tokens // ROW, len_ref, count_ref, cols_of, packed, dmixed, lse_ref, table_ref, toep, diag, out_ref, dbias_ref
    )
    for copy in later:
        copy.wait()
    for part in range(3):
        at = part * D
        total[at : at + start] = dot(first[:, part * start : (part + 1) * start], normed[...], TN)
        total[at + start : at + D] = dot(out_ref[:, part * width : (part + 1) * width], normed[...], TN)
    for core, kept, out in ((1, other, other_out), (0, own, own_out)):

        @pl.loop(0, 32)
        def _(i):
            half, plane, z = i // 16, i // 4 % 4, i % 4
            owner = me_ref[0] ^ (z * 8 + plane * 2 + core)
            row = pl.multiple_of(owner * SHARD + half * HALF, 16)
            to = pl.multiple_of(i * HALF, 16)
            kept[pl.ds(to, HALF), :] = total[pl.ds(row, HALF), :].astype(kept.dtype)

        pltpu.make_async_copy(kept, out, out_sems.at[core]).start()
    for core, kept, out in ((1, other, other_out), (0, own, own_out)):
        pltpu.make_async_copy(kept, out, out_sems.at[core]).wait()


def last_back_call(me, lengths, counts, lse, table, normed, first, grad_out, packed, dmixed):
    tokens = normed.shape[0]
    anywhere = pl.BlockSpec(memory_space=pl.ANY)
    inside = pl.BlockSpec(memory_space=pltpu.VMEM)
    width = (PAIRS - FIRST) * WIDE
    return pl.pallas_call(
        last_back_kernel,
        grid_spec=pltpu.PrefetchScalarGridSpec(
            num_scalar_prefetch=3,
            grid=(),
            in_specs=[inside] * 2 + [anywhere] * 5,
            out_specs=[inside] * 2 + [anywhere] * 2,
            scratch_shapes=[
                pltpu.VMEM((tokens, 3 * width), BF16),
                pltpu.VMEM((tokens, width), BF16),
                pltpu.VMEM((tokens, D), BF16),
                pltpu.VMEM((tokens, 3 * FIRST * WIDE), BF16),
                pltpu.VMEM((2 * D, D), F32),
                pltpu.VMEM((2 * D, D), BF16),
                pltpu.VMEM((4 * D, D), F32),
                pltpu.VMEM((2, SUB, TOEP), F32),
                pltpu.VMEM((2, SUB, TOEP), F32),
                pltpu.SemaphoreType.DMA((7,)),
                pltpu.SemaphoreType.DMA((2,)),
            ],
        ),
        out_shape=[
            jax.ShapeDtypeStruct((tokens, 3 * width), BF16),
            jax.ShapeDtypeStruct((PAIRS - FIRST, 2, SPAN), F32),
            jax.ShapeDtypeStruct((2 * D, D), F32),
            jax.ShapeDtypeStruct((2 * D, D), BF16),
        ],
        compiler_params=params(),
        cost_estimate=cost(10e9, 30e6, 4e6),
        name="last_back",
    )(me, lengths, counts, lse, table, normed, first, grad_out, packed, dmixed)


def feed_tile(second, grad, up, down):
    u = dot(second, up, NT)
    square = u * u
    t = jnp.tanh(0.7978845608 * u * (1.0 + 0.044715 * square))
    plus = 0.5 * (1.0 + t)
    slope = plus + (0.5 * 0.7978845608) * u * (1.0 - t * t) * (1.0 + 3 * 0.044715 * square)
    dh = dot(grad, down, NT).astype(BF16).astype(F32)
    return (u * plus).astype(BF16), (dh * slope).astype(BF16)


def weights_of(refs):
    return [jnp.concatenate([ref[...] for ref in refs[i : i + 4]], axis=0) for i in (0, 4)]


def feed_kernel(parts, *refs):
    up, down = weights_of(refs[:8])
    second_ref, grad_ref, *refs, back_ref, hidden_ref, dpre_ref = refs[8:]
    hidden, du = feed_tile(second_ref[...], grad_ref[...], up, down)
    hidden_ref[...] = hidden
    dpre_ref[...] = du
    back = dot(du, up, NN)
    back_ref[...] = back + refs[0][...] if parts else back


def feed_call(weights, second, out_grad, start=None):
    tokens = second.shape[0]
    flat = tiles(TILE, D)
    low_flat = jax.ShapeDtypeStruct((tokens, D), BF16)
    more = [] if start is None else [start]
    return pl.pallas_call(
        functools.partial(feed_kernel, len(more)),
        grid=(tokens // TILE,),
        in_specs=[piece_block()] * 8 + [flat, flat] + [flat] * len(more),
        out_specs=[flat, flat, flat],
        out_shape=[jax.ShapeDtypeStruct((tokens, D), F32), low_flat, low_flat],
        compiler_params=params(),
        cost_estimate=cost(6 * tokens * D * D, 15e6, tokens * D),
        name="feed",
    )(*weights, second, out_grad, *more)


def feed_sum_kernel(parts, *refs):
    weights = refs[:8]
    second_ref, grad_ref, second_other, grad_other, hidden_other, dpre_other, *refs = refs[8:]
    back_ref, hidden_ref, out_ref, dpre = refs[-4:]
    step = pl.program_id(0)
    count = second_ref.shape[0] // TILE

    @pl.when(step < count)
    def _():
        at = pl.ds(pl.multiple_of(step * TILE, TILE), TILE)
        up, down = weights_of(weights)
        hidden, du = feed_tile(second_ref[at, :], grad_ref[at, :], up, down)
        hidden_ref[at, :] = hidden
        dpre[at, :] = du
        back = dot(du, up, NN)
        back_ref[...] = back + refs[0][...] if parts else back

    @pl.when(step == count)
    def _():
        out_ref[0] = dot(dpre[...], second_ref[...], TN) + dot(dpre_other[...], second_other[...], TN)

    @pl.when(step == count + 1)
    def _():
        out_ref[0] = dot(hidden_ref[...], grad_ref[...], TN) + dot(hidden_other[...], grad_other[...], TN)


def feed_sum_call(weights, second, out_grad, second_other, grad_other, hidden_other, dpre_other, start=None):
    tokens = second.shape[0]
    count = tokens // TILE
    flat = pl.BlockSpec((tokens, D), lambda i: (0, 0), pipeline_mode=pl.Buffered(1))
    tile = pl.BlockSpec((TILE, D), lambda i: (jnp.minimum(i, count - 1), 0))
    more = [] if start is None else [start]
    return pl.pallas_call(
        functools.partial(feed_sum_kernel, len(more)),
        grid=(count + 2,),
        in_specs=[piece_block()] * 8 + [flat] * 6 + [tile] * len(more),
        out_specs=[tile, whole((tokens, D)), pl.BlockSpec((1, D, D), lambda i: (jnp.maximum(i - count, 0), 0, 0))],
        out_shape=[
            jax.ShapeDtypeStruct((tokens, D), F32),
            jax.ShapeDtypeStruct((tokens, D), BF16),
            jax.ShapeDtypeStruct((2, D, D), F32),
        ],
        scratch_shapes=[pltpu.VMEM((tokens, D), BF16)],
        compiler_params=params(),
        cost_estimate=cost(14 * tokens * D * D, 30e6, tokens * D),
        name="feed_sum",
    )(*weights, second, out_grad, second_other, grad_other, hidden_other, dpre_other, *more)


def output_part(refs):
    total = None
    for half, hidden in enumerate(refs[:2]):
        down = jnp.concatenate([ref[...] for ref in refs[2 + 4 * half : 6 + 4 * half]], axis=0)
        part = dot(hidden[...], down, NN)
        total = part if total is None else total + part
    return total


def output_other_kernel(*refs):
    refs[-1][...] = output_part(refs)


def output_kernel(*refs):
    middle_ref, got_ref, out_ref = refs[10:]
    out_ref[...] = (middle_ref[...] + (output_part(refs) + got_ref[...])).astype(BF16)


def output_call(hiddens, weights, more=()):
    tokens = hiddens[0].shape[0]
    return pl.pallas_call(
        output_kernel if more else output_other_kernel,
        grid=(tokens // TILE,),
        in_specs=[tiles(TILE, D)] * 2 + [piece_block()] * 8 + [tiles(TILE, D)] * len(more),
        out_specs=tiles(TILE, D),
        out_shape=jax.ShapeDtypeStruct((tokens, D), BF16 if more else F32),
        compiler_params=params(),
        cost_estimate=cost(4 * tokens * D * D, 12e6),
        name="output",
    )(*hiddens, *weights, *more)


def input_back_kernel(first_ref, last_ref, x_ref, dmiddle_ref, gain_ref, weight_ref, dx_ref, dgain_ref):
    step = pl.program_id(0)
    da = jnp.zeros(dx_ref.shape, F32)
    cut = FIRST * WIDE
    for part in range(3):
        da += dot(first_ref[:, part * cut : (part + 1) * cut], weight_ref[part * D : part * D + cut, :], NN)
        rest = D - cut
        da += dot(last_ref[:, part * rest : (part + 1) * rest], weight_ref[part * D + cut : (part + 1) * D, :], NN)
    x = x_ref[...].astype(F32)
    scale = lax.rsqrt(jnp.mean(x * x, axis=-1, keepdims=True) + EPS)
    dm = da * gain_ref[0:1, :]
    inner = jnp.mean(dm * x, axis=-1, keepdims=True)
    dx_ref[...] = dmiddle_ref[...] + scale * dm - x * (scale * scale * scale * inner)
    dgain = jnp.sum(da * x * scale, axis=0, keepdims=True)

    @pl.when(step == 0)
    def _():
        dgain_ref[...] = dgain

    @pl.when(step > 0)
    def _():
        dgain_ref[...] += dgain


def input_back_call(first, last, x, dmiddle, gains, weight):
    tokens = x.shape[0]
    return pl.pallas_call(
        input_back_kernel,
        grid=(tokens // TILE,),
        in_specs=[
            tiles(TILE, first.shape[1]),
            tiles(TILE, last.shape[1]),
            tiles(TILE, D),
            tiles(TILE, D),
            whole((2, D)),
            whole((3 * D, D)),
        ],
        out_specs=[tiles(TILE, D), whole((1, D))],
        out_shape=[jax.ShapeDtypeStruct((tokens, D), F32), jax.ShapeDtypeStruct((1, D), F32)],
        compiler_params=params(),
        cost_estimate=cost(2 * tokens * D * 3 * D, 18e6),
        name="input_back",
    )(first, last, x, dmiddle, gains, weight)


def adam_update(param, grad, first, second, rate):
    first_new = BETA_ONE * first + (1.0 - BETA_ONE) * grad
    second_new = BETA_TWO * second + (1.0 - BETA_TWO) * grad * grad
    first_hat = first_new / (1.0 - BETA_ONE**STEP)
    second_hat = second_new / (1.0 - BETA_TWO**STEP)
    param_new = param - rate * (first_hat / (jnp.sqrt(second_hat) + ADAM_EPS) + DECAY * param)
    return (param_new, first_new, second_new)


AXES = ("tree", "rest")
CORE, Y, X, Z = 1, 2, 4, 8


def swap(value, bits):
    return lax.ppermute(value, "tree", [(i, i ^ bits) for i in range(32)])


def tie(values, after):
    return list(lax.optimization_barrier(tuple(values) + tuple(after))[: len(values)])


def gather_z(shard):
    return [shard] + [swap(shard, k * Z) for k in (1, 2, 3)]


def gather_halves(line, first=0):
    return [jnp.concatenate([p[i : i + HALF] for p in line]) for i in (first, first + HALF)]


def gather_plane(halves):
    return [swap(halves[0], X), swap(halves[1], Y)]


def gather_rest(halves, turned):
    return [swap(halves[0], Y), swap(turned[0], Y), swap(halves[1], X), swap(turned[1], X)]


def gathered(halves, turned, rest):
    return [halves[0], rest[0], turned[0], rest[1], halves[1], turned[1], rest[2], rest[3]]


def gather_core(pieces):
    return [swap(p, CORE) for p in pieces]


def low(value):
    return value.astype(BF16)


def added(value, got):
    return value if got is None else value + got.astype(F32)


def reduce_plane(own, got=None):
    shape = (2, 2, 2, 4, HALF, D)
    own = own.reshape(shape)
    got = None if got is None else got.reshape(shape)

    def part(*at):
        return added(own[at], None if got is None else got[at])

    every = slice(None)
    return [part(0, every, 0), part(1, 0)], [low(part(0, every, 1)), low(part(1, 1))]


def swap_plane(sends):
    return [swap(sends[0], Y), swap(sends[1], X)]


def reduce_rest(keep, got):
    parts = [[added(k[i], g[i]) for k, g in zip(keep, got)] for i in range(2)]
    return parts[0], [low(part) for part in parts[1]]


def swap_rest(sends):
    return [swap(sends[0], X), swap(sends[1], Y)]


def line_kernel(one_ref, two_ref, got_one, got_two, *outs):
    for k, out in enumerate(outs):
        out[:HALF] = (one_ref[k] + got_one[k].astype(F32)).astype(out.dtype)
        out[HALF:] = (two_ref[k] + got_two[k].astype(F32)).astype(out.dtype)


def reduce_line(keep, got):
    shape = (SHARD, D)
    outs = pl.pallas_call(
        line_kernel,
        out_shape=[jax.ShapeDtypeStruct(shape, F32)] + [jax.ShapeDtypeStruct(shape, BF16)] * 3,
        compiler_params=params(),
        cost_estimate=cost(1e6, 6e6),
        name="line",
    )(*keep, *got)
    return outs[0], list(outs[1:])


def swap_line(sends):
    return [swap(send, k * Z) for k, send in zip((1, 2, 3), sends)]


def reduced(keep, got):
    return keep + got[0].astype(F32) + got[1].astype(F32) + got[2].astype(F32)


def on_device(
    layer_input, out_grad, matrices, mat_first, mat_second, mat_ema, gains, gain_first, gain_second,
    rel_bias, bias_first, bias_second, bucket_len, item_count, bucket_table,
):
    rest = lax.axis_size("rest")
    shards = jnp.swapaxes(matrices, 1, 2).astype(BF16)
    if rest > 1:
        shards = lax.all_gather(shards, "rest", axis=1, tiled=True)
    shard_f = jnp.concatenate(
        [shards[1, :HALF], shards[2, :HALF], shards[1, HALF:], shards[2, HALF:]]
    )
    where = lax.axis_index("tree").astype(jnp.int32)
    me = where.reshape(1)
    flipped = jnp.concatenate([bucket_table[::-1], jnp.full((1,), -1, jnp.int32)])
    onehot = (flipped[None, :] == jnp.arange(BUCKETS, dtype=jnp.int32)[:, None]).astype(F32)
    table = jnp.dot(rel_bias.T, onehot, precision=lax.Precision.HIGHEST).reshape(PAIRS, 2, SPAN)

    line_w = gather_z(shards[0])
    halves_w = gather_halves(line_w)
    turned_w = gather_plane(halves_w)
    (shard_f,) = tie([shard_f], halves_w)
    line_f = gather_z(shard_f)
    near_w = [jnp.concatenate([half, turned]) for half, turned in zip(halves_w, turned_w)]
    far_w = [swap(near_w[0], Y), swap(near_w[1], X)]
    own_w = [near_w[0], far_w[0], near_w[1], far_w[1]]
    (own_w[0], own_w[2]) = tie(near_w, far_w)
    other_w = gather_core(own_w)
    halves_a = tie(gather_halves(line_f, 0), far_w)
    halves_b = tie(gather_halves(line_f, 2 * HALF), far_w)
    turned_a = gather_plane(halves_a)
    turned_b = gather_plane(halves_b)
    (late_input,) = tie([layer_input], halves_a + halves_b)
    normed, packed, attn_weight, stats, mixed_first = first_forward_call(
        me, bucket_len, item_count, own_w + other_w, late_input, gains, table
    )
    (grad_send,) = tie([out_grad], [normed])
    grad_other = swap(grad_send, CORE)
    turned_a = tie(turned_a, [normed])
    turned_b = tie(turned_b, [normed])
    rest_a = gather_rest(halves_a, turned_a)
    (mixed_first,) = tie([mixed_first], turned_a + turned_b)
    lse, mixed, middle, second = last_forward_call(
        bucket_len, item_count, layer_input, gains, table, mixed_first, stats, attn_weight, packed
    )

    rest_a = tie(rest_a, [lse])
    own_a = gathered(halves_a, turned_a, rest_a)
    halves_b = tie(halves_b, rest_a)
    rest_b = gather_rest(halves_b, turned_b)
    (second,) = tie([second], rest_a)
    second_other = swap(second, CORE)
    back_other, hidden_oa, dpre_oa = feed_call(own_a, second_other, grad_other)
    (second_a,) = tie([second], [dpre_oa])
    back, hidden_a, grad_a = feed_sum_call(own_a, second_a, out_grad, second_other, grad_other, hidden_oa, dpre_oa)
    rest_b = tie(rest_b, [grad_a])
    own_b = gathered(halves_b, turned_b, rest_b)
    keep_a, send_a = reduce_plane(grad_a)
    (second_other_b,) = tie([second_other], send_a + rest_b)
    got_a = swap_plane(send_a)
    back_other, hidden_ob, dpre_ob = feed_call(own_b, second_other_b, grad_other, back_other)
    back_got = swap(back_other, CORE)
    (second_b,) = tie([second], [dpre_ob])
    back, hidden_b, grad_b = feed_sum_call(
        own_b, second_b, out_grad, second_other_b, grad_other, hidden_ob, dpre_ob, back
    )

    got_a = tie(got_a, [grad_b])
    keep_a, send_a = reduce_rest(keep_a, got_a)
    got_a = swap_rest(send_a)
    keep_b, send_b = reduce_plane(grad_b)
    got_b = swap_plane(send_b)
    (back,) = tie([back], send_a + send_b + [back_got])
    dgain_two, first_d, lines_a, dmiddle, dmixed, grad_out = first_back_call(
        bucket_len, item_count, back, back_got, middle, out_grad, mixed, gains, lse, table, attn_weight, packed
    )
    got_a = tie(got_a, [dmixed])
    got_b = tie(got_b, [dmixed])
    keep_a, send_a = reduce_line(keep_a, got_a)
    got_a = swap_line(send_a)
    keep_b, send_b = reduce_rest(keep_b, got_b)
    got_b = swap_rest(send_b)
    (dmixed,) = tie([dmixed], send_a + send_b)
    last_d, lines_b, mine_w, other_w = last_back_call(
        me, bucket_len, item_count, lse, table, normed, first_d, grad_out, packed, dmixed
    )

    got_b = tie(got_b, [last_d])
    (other_w,) = tie([other_w], got_a + got_b)
    core_w = swap(other_w, CORE)
    keep_b, send_b = reduce_line(keep_b, got_b)
    got_b = swap_line(send_b)
    (core_w,) = tie([core_w], send_b)
    keep_w, send_w = reduce_plane(mine_w, core_w)
    got_w = swap_plane(send_w)
    (last_e,) = tie([last_d], send_w)
    input_grad, dgain_one = input_back_call(first_d, last_e, layer_input, dmiddle, gains, attn_weight)
    got_w = tie(got_w, [input_grad])
    keep_w, send_w = reduce_rest(keep_w, got_w)
    got_w = swap_rest(send_w)

    lines_a, lines_b, dgain_one = tie([lines_a, lines_b, dgain_one], send_w)
    bias_local = jnp.dot(
        onehot, jnp.concatenate([lines_a, lines_b]).reshape(HEADS, SPAN).T, precision=lax.Precision.HIGHEST
    )
    small = jnp.concatenate([dgain_one.reshape(-1), dgain_two.reshape(-1), bias_local.reshape(-1)]).reshape(-1, 128)
    small_got = swap(small, CORE)
    (hidden_late,) = tie([hidden_oa], send_w + [small] + got_b)
    downs = own_a[4:] + own_b[4:]
    output_other = output_call([hidden_late, hidden_ob], downs)
    got_w = tie(got_w, [output_other])
    small = small + tie([small_got], [output_other])[0]
    keep_w, send_w = reduce_line(keep_w, got_w)
    got_w = swap_line(send_w)
    small_y, small_x, small_xy = (swap(small, bits) for bits in (Y, X, X | Y))
    (output_other,) = tie([output_other], send_w)
    output_got = swap(output_other, CORE)
    (hidden_last,) = tie([hidden_a], [output_other, small])
    layer_output = output_call([hidden_last, hidden_b], downs, (middle, output_got))
    small_y, small_x, small_xy, *got_w = tie([small_y, small_x, small_xy] + got_w, [layer_output])
    small = (small + small_y) + (small_x + small_xy)
    small = (small + swap(small, Z)) + (swap(small, 2 * Z) + swap(small, 3 * Z))
    small = small.reshape(-1)
    sum_a, sum_b, sum_w = reduced(keep_a, got_a), reduced(keep_b, got_b), reduced(keep_w, got_w)
    sum_f = jnp.stack([sum_a, sum_b]).reshape(2, 2, HALF, D).swapaxes(0, 1)

    summed = jnp.concatenate([sum_w.reshape(1, SHARD, D), sum_f.reshape(2, SHARD, D)])
    if rest > 1:
        small = lax.psum(small, "rest")
        summed = lax.psum_scatter(summed, "rest", scatter_dimension=1, tiled=True)
    gain_grad = small[: 2 * D].reshape(2, D)
    bias_grad = small[2 * D :].reshape(BUCKETS, HEADS)
    mat_grad = jnp.swapaxes(summed, 1, 2)
    mat_new, mat_first_new, mat_second_new = adam_update(
        matrices, mat_grad, mat_first, mat_second, RATE
    )
    mat_ema_new = EMA_KEEP * mat_ema + (1.0 - EMA_KEEP) * mat_new
    gain_new, gain_first_new, gain_second_new = adam_update(
        gains, gain_grad, gain_first, gain_second, RATE_SMALL
    )
    bias_new, bias_first_new, bias_second_new = adam_update(
        rel_bias, bias_grad, bias_first, bias_second, RATE_SMALL
    )
    return (
        layer_output, input_grad, mat_grad, mat_new, mat_first_new, mat_second_new, mat_ema_new,
        gain_grad, gain_new, gain_first_new, gain_second_new,
        bias_grad, bias_new, bias_first_new, bias_second_new,
    )


def solution(mesh):
    fine = Mesh(mesh.devices.reshape(32, -1), AXES)
    rows = P(AXES, None)
    columns = P(None, None, AXES)
    return jax.shard_map(
        on_device,
        mesh=fine,
        in_specs=(rows, rows) + (columns,) * 4 + (P(),) * 6 + (P(AXES), P(AXES), P()),
        out_specs=(rows, rows) + (columns,) * 5 + (P(),) * 8,
        check_vma=False,
    )
```

time: 689 us -> 310 us (0.45)
  waiting for transfers between devices: 442 us -> 32.4 us
  starting transfers between devices: 0.42 us -> 77.3 us
  blocking collectives: 40.3 us -> 0 us
  between operations: 14.9 us -> 2.67 us
    reduce_scatter x3 -> x0, waiting for transfers between devices: 295 us -> none  [scatter(): return lax.psum_scatter(value, AXES, scatter_dimension=0, tiled=True)]
    all_gather x3 -> x0, waiting for transfers between devices: 145 us -> none  [on_device(): lax.all_gather(shards[i], AXES, axis=0, tiled=True)]
    ppermute x0 -> x59, starting transfers between devices: none -> 77.3 us  [swap(): return lax.ppermute(value, 'tree', [(i, i ^ bits) for i in range(32)])]
    psum x1 -> x0, blocking collectives: 40.3 us -> none  [on_device(): gain_grad, bias_grad = lax.psum((gain_local, bias_local), AXES)]
    ppermute x0 -> x59, waiting for transfers between devices: none -> 32.4 us  [swap(): return lax.ppermute(value, 'tree', [(i, i ^ bits) for i in range(32)])]
    slice x4 -> x6, local copies, waits for them, and re-layouts: 8.47 us -> 0.12 us  [the longest x5 0.11 us: gather_halves(): p[i:i + HALF]]
    add x0 -> x10, other arithmetic: none -> 8.11 us  [the longest x5 6.92 us: added(): return value if got is None else value + got.astype(F32)]
    concatenate x2 -> x6, other arithmetic: 8.03 us -> 0.17 us  [the longest x4 0.13 us: gather_halves(): jnp.concatenate([p[i:i + HALF] for p in line])]
  transfers between devices with their start and end apart: 6 -> 59, of which waited for: 6 -> 12; matrix products, arithmetic and copies ran while one was open for 4% -> 7% of each run, Pallas kernels for 15% -> 48%
where the time goes in v2:
time: 310 us; the launch traced here: 306 us
  Pallas kernels  159 us (51%)
  starting transfers between devices  77.3 us (25%)
  waiting for transfers between devices  32.4 us (10%)
  local copies, waits for them, and re-layouts  17.5 us (6%)
  other arithmetic  16.9 us (5%)
    ppermute x59, starting transfers between devices, swap(): return lax.ppermute(value, 'tree', [(i, i ^ bits) for i in range(32)])  77.3 us
    pallas_call x2, Pallas kernels, feed_sum_call(): pl.pallas_call(functools.partial(feed_sum_kernel, len(more)), grid=(count...  36 us
    ppermute x59, waiting for transfers between devices, swap(): return lax.ppermute(value, 'tree', [(i, i ^ bits) for i in range(32)])  32.4 us
    pallas_call x1, Pallas kernels, first_back_call(): pl.pallas_call(first_back_kernel, grid_spec=pltpu.PrefetchScalarGridSpec(...  26.3 us
    pallas_call x1, Pallas kernels, last_back_call(): pl.pallas_call(last_back_kernel, grid_spec=pltpu.PrefetchScalarGridSpec(n...  18.9 us
    pallas_call x2, Pallas kernels, feed_call(): pl.pallas_call(functools.partial(feed_kernel, len(more)), grid=(tokens //...  16.8 us
    pallas_call x1, Pallas kernels, first_forward_call(): pl.pallas_call(first_forward_kernel, grid_spec=pltpu.PrefetchScalarGridSp...  15.7 us
    pallas_call x2, Pallas kernels, output_call(): pl.pallas_call(output_kernel if more else output_other_kernel, grid=(toke...  14.6 us
  transfers between devices with their start and end apart: 59, of which 12 were waited for; matrix products, arithmetic and copies ran while one was open for 7% of the time, Pallas kernels for 48%

profile of v2, /device:TPU:0, one launch (start us, length us, event | category | flops | bytes accessed | tf_op | source)
XLA Modules:
  0.0 306.1 jit_solution(14224841775667162817)
XLA Ops:
  1.9 5.1 %collective-permute-start.2 = (bf16[96,768]{1,0:T(8,128)(2,1)S(1)}, bf16[96,768]{1,0:T(8,128)(2,1)S(1)}, u32[]{:S(2)}, u32[]{:S(2)}) collective-permute-start(bf16[96,768]{1,0:T(8,128)(2,1)S(1)} %slice_bitcast_fusion.16), channel_id=1, source_target_pairs={{0,24},{1,25},{2,26},{3,27},{4,28},{5,29},{6,30},{7,31},{8,16},{9,... | collective-permute-start | bytes 442376 | tf_op jit(solution)/shard_map/ppermute | solution.py:781
  8.5 8.0 %collective-permute-done = bf16[96,768]{1,0:T(8,128)(2,1)S(1)} collective-permute-done((bf16[96,768]{1,0:T(8,128)(2,1)S(1)}, bf16[96,768]{1,0:T(8,128)(2,1)S(1)}, u32[]{:S(2)}, u32[]{:S(2)}) %collective-permute-start) | collective-permute-done | bytes 147488 | tf_op jit(solution)/shard_map/ppermute | solution.py:781
  17.2 2.3 collective-permute-done.1
  20.8 1.6 collective-permute-start.8
  22.4 1.6 collective-permute-start.6
  24.1 2.6 collective-permute-start.5
  26.7 2.3 collective-permute-done.8
  29.0 1.6 collective-permute-start.9
  36.1 3.0 collective-permute-start.3
  39.1 3.9 %collective-permute-done.9.refs_3_ = bf16[384,768]{1,0:T(8,128)(2,1)} collective-permute-done((bf16[384,768]{1,0:T(8,128)(2,1)S(1)}, bf16[384,768]{1,0:T(8,128)(2,1)}, u32[]{:S(2)}, u32[]{:S(2)}) %collective-permute-start.9) | collective-permute-done | bytes 589856 | tf_op jit(solution)/shard_map/ppermute | solution.py:781
  43.0 1.8 collective-permute-done.7.refs_1_
  45.3 4.8 %collective-permute-done.4 = bf16[192,768]{1,0:T(8,128)(2,1)S(1)} collective-permute-done((bf16[192,768]{1,0:T(8,128)(2,1)S(1)}, bf16[192,768]{1,0:T(8,128)(2,1)S(1)}, u32[]{:S(2)}, u32[]{:S(2)}) %collective-permute-start.4) | collective-permute-done | bytes 294944 | tf_op jit(solution)/shard_map/ppermute | solution.py:781
  52.9 1.5 collective-permute-start.20
  55.3 15.7 %first_forward.1 = (bf16[1024,768]{1,0:T(8,128)(2,1)}, bf16[1024,2304]{1,0:T(8,128)(2,1)}, bf16[3072,768]{1,0:T(8,128)(2,1)}, f32[1024,128]{1,0:T(8,128)}, bf16[1024,384]{1,0:T(8,128)(2,1)}) custom-call(s32[1]{0:T(128)} %bitcast.8.me_ref, s32[2]{0:T(128)} %dynamic-slice.3.len_ref, s32[2]{0:T(128)} %dynamic-slice.7.count_ref, ...), custom_call_target="tpu_custom_call" | custom-call | flops 12000000000 | bytes 30000000 | tf_op jit(solution)/shard_map/first_forward/pallas_call | solution.py:211
  71.0 2.3 collective-permute-start.18
  73.3 2.3 collective-permute-start.17
  75.6 2.0 collective-permute-start.19
  77.6 14.1 %last_forward.1 = (f32[1024,128]{1,0:T(8,128)}, bf16[1024,768]{1,0:T(8,128)(2,1)}, f32[1024,768]{1,0:T(8,128)}, bf16[1024,768]{1,0:T(8,128)(2,1)}) custom-call(s32[2]{0:T(128)} %dynamic-slice.3.len_ref, s32[2]{0:T(128)} %dynamic-slice.7.count_ref, bf16[1024,768]{1,0:T(8,128)(2,1)} %x_ref.3, f32[2,768]{1,0:T(2,128)} %gain_ref.5, ...), custom_call_target="tpu_custom_call" | custom-call | flops 8000000000 | bytes 20000000 | tf_op jit(solution)/shard_map/last_forward/pallas_call | solution.py:283
  92.4 2.0 collective-permute-start.22
  96.5 2.0 collective-permute-start.26
  99.7 8.0 %feed.2 = (f32[1024,768]{1,0:T(8,128)}, bf16[1024,768]{1,0:T(8,128)(2,1)}, bf16[1024,768]{1,0:T(8,128)(2,1)}) custom-call(bf16[192,768]{1,0:T(8,128)(2,1)} %copy-done.23, bf16[192,768]{1,0:T(8,128)(2,1)} %copy-done.53, bf16[192,768]{1,0:T(8,128)(2,1)} %copy-done.52, bf16[192,768]{1,0:T(8,128)(2,1)} %copy-done.55, bf16[192,768]{1,0:T(8,128)(2,1)} %copy-done.4, ...), custom_call_target="tpu_custom_call" | custom-call | flops 3623878656 | bytes 15000000 | tf_op jit(solution)/shard_map/feed/pallas_call | solution.py:629
  107.8 18.0 %feed_sum.2 = (f32[1024,768]{1,0:T(8,128)}, bf16[1024,768]{1,0:T(8,128)(2,1)}, f32[2,768,768]{2,1,0:T(8,128)}) custom-call(bf16[192,768]{1,0:T(8,128)(2,1)} %copy-done.23, bf16[192,768]{1,0:T(8,128)(2,1)} %copy-done.53, bf16[192,768]{1,0:T(8,128)(2,1)} %copy-done.52, bf16[192,768]{1,0:T(8,128)(2,1)} %copy-done.55, bf16[192,768]{1,0:T(8,128)(2,1)} %copy-done.4, ...), custom_call_target="tpu_custom_call" | custom-call | flops 8455716864 | bytes 30000000 | tf_op jit(solution)/shard_map/feed_sum/pallas_call | solution.py:673
  129.3 8.7 %feed.3 = (f32[1024,768]{1,0:T(8,128)}, bf16[1024,768]{1,0:T(8,128)(2,1)}, bf16[1024,768]{1,0:T(8,128)(2,1)}) custom-call(bf16[192,768]{1,0:T(8,128)(2,1)} %copy-done.21, bf16[192,768]{1,0:T(8,128)(2,1)} %collective-permute-done.24.refs_1_, bf16[192,768]{1,0:T(8,128)(2,1)} %copy-done.51, bf16[192,768]{1,0:T(8,128)(2,1)} %copy-done.54, ...), custom_call_target="tpu_custom_call" | custom-call | flops 3623878656 | bytes 15000000 | tf_op jit(solution)/shard_map/feed/pallas_call | solution.py:629
  140.6 18.0 %feed_sum.3 = (f32[1024,768]{1,0:T(8,128)}, bf16[1024,768]{1,0:T(8,128)(2,1)}, f32[2,768,768]{2,1,0:T(8,128)}) custom-call(bf16[192,768]{1,0:T(8,128)(2,1)} %copy-done.21, bf16[192,768]{1,0:T(8,128)(2,1)} %collective-permute-done.24.refs_1_, bf16[192,768]{1,0:T(8,128)(2,1)} %copy-done.51, bf16[192,768]{1,0:T(8,128)(2,1)} %copy-done.54, ...), custom_call_target="tpu_custom_call" | custom-call | flops 8455716864 | bytes 30000000 | tf_op jit(solution)/shard_map/feed_sum/pallas_call | solution.py:673
  163.1 2.5 fusion.19
  168.0 26.3 %first_back.1 = (f32[1,768]{1,0:T(1,128)}, bf16[1024,1536]{1,0:T(8,128)(2,1)}, f32[4,2,1024]{2,1,0:T(2,128)}, f32[1024,768]{1,0:T(8,128)}, bf16[1024,768]{1,0:T(8,128)(2,1)}, /*index=5*/f32[768,768]{1,0:T(8,128)}) custom-call(s32[2]{0:T(128)} %dynamic-slice.3.len_ref, s32[2]{0:T(128)} %dynamic-slice.7.count_ref, ...), custom_call_target="tpu_custom_call" | custom-call | flops 15000000512 | bytes 30000000 | tf_op jit(solution)/shard_map/first_back/pallas_call | solution.py:473
  195.1 2.3 line.3
  197.4 2.9 collective-permute-start.36
  200.3 1.5 collective-permute-start.37
  203.0 7.9 %collective-permute-start.39 = (bf16[4,48,768]{2,1,0:T(8,128)(2,1)S(1)}, bf16[4,48,768]{2,1,0:T(8,128)(2,1)S(1)}, u32[]{:S(2)}, u32[]{:S(2)}) collective-permute-start(bf16[4,48,768]{2,1,0:T(8,128)(2,1)S(1)} %get-tuple-element.267), channel_id=1, source_target_pairs={{0,2},{1,3},{2,0},{3,1},{4,6},{5,7},{6,4},{7,5},{8,10},{9,11},{10,... | collective-permute-start | bytes 884744 | tf_op jit(solution)/shard_map/ppermute | solution.py:781
  211.0 18.9 %last_back.1 = (bf16[1024,768]{1,0:T(8,128)(2,1)}, f32[2,2,1024]{2,1,0:T(2,128)}, f32[1536,768]{1,0:T(8,128)}, bf16[1536,768]{1,0:T(8,128)(2,1)}) custom-call(s32[1]{0:T(128)} %bitcast.8.me_ref, s32[2]{0:T(128)} %dynamic-slice.3.len_ref, s32[2]{0:T(128)} %dynamic-slice.7.count_ref, f32[1024,128]{1,0:T(8,128)} %get-tuple-element.136.lse_ref, ...), custom_call_target="tpu_custom_call" | custom-call | flops 10000000000 | bytes 30000000 | tf_op jit(solution)/shard_map/last_back/pallas_call | solution.py:567
  230.8 2.3 line.4
  233.1 1.8 collective-permute-done.40
  234.9 2.9 fusion.3
  238.3 3.5 %collective-permute-start.41 = (bf16[2,4,48,768]{3,2,1,0:T(8,128)(2,1)}, bf16[2,4,48,768]{3,2,1,0:T(8,128)(2,1)S(1)}, u32[]{:S(2)}, u32[]{:S(2)}) collective-permute-start(bf16[2,4,48,768]{3,2,1,0:T(8,128)(2,1)} %get-tuple-element.264), channel_id=1, source_target_pairs={{0,2},{1,3},{2,0},{3,1},{4,6},{5,7},{6,4},{7,5},{8,10},{9,11},{10,... | collective-permute-start | bytes 1769480 | tf_op jit(solution)/shard_map/ppermute | solution.py:781
  243.9 3.8 %collective-permute-start.45 = (bf16[96,768]{1,0:T(8,128)(2,1)}, bf16[96,768]{1,0:T(8,128)(2,1)}, u32[]{:S(2)}, u32[]{:S(2)}) collective-permute-start(bf16[96,768]{1,0:T(8,128)(2,1)} %get-tuple-element.188), channel_id=1, source_target_pairs={{0,24},{1,25},{2,26},{3,27},{4,28},{5,29},{6,30},{7,31},{8,16},{9,... | collective-permute-start | bytes 442376 | tf_op jit(solution)/shard_map/ppermute | solution.py:781
  247.7 9.8 %input_back.1 = (f32[1024,768]{1,0:T(8,128)}, f32[1,768]{1,0:T(1,128)}) custom-call(bf16[1024,1536]{1,0:T(8,128)(2,1)} %get-tuple-element.169.first_in.first_ref, bf16[1024,768]{1,0:T(8,128)(2,1)} %get-tuple-element.190.last_ref, bf16[1024,768]{1,0:T(8,128)(2,1)} %x_ref.3, f32[1024,768]{1,0:T(8,128)} %get-tuple-element.191.dmiddle_ref, f32[2,768]{1,0:T(2,128)} %gain_ref.5, ...), custom_call_target="tpu_custom_call" | custom-call | flops 3623878656 | bytes 18000000 | tf_op jit(solution)/shard_map/input_back/pallas_call | solution.py:748
  257.5 2.0 fusion.6
  259.5 1.9 collective-permute-start.47
  263.1 6.9 %output.2 = f32[1024,768]{1,0:T(8,128)} custom-call(bf16[1024,768]{1,0:T(8,128)(2,1)} %get-tuple-element.202.refs_12_.refs_0_, bf16[1024,768]{1,0:T(8,128)(2,1)} %get-tuple-element.160.refs_12_.refs_1_, bf16[192,768]{1,0:T(8,128)(2,1)} %copy-done.4, bf16[192,768]{1,0:T(8,128)(2,1)} %copy-done.8, bf16[192,768]{1,0:T(8,128)(2,1)} %copy-done.10, ...), custom_call_target="tpu_custom_call" | custom-call | flops 2415919104 | bytes 12000000 | tf_op jit(solution)/shard_map/output/pallas_call | solution.py:710
  270.9 2.3 line.5
  274.9 3.5 %collective-permute-done.48 = f32[15,128]{1,0:T(8,128)S(1)} collective-permute-done((f32[15,128]{1,0:T(8,128)S(1)}, f32[15,128]{1,0:T(8,128)S(1)}, u32[]{:S(2)}, u32[]{:S(2)}) %collective-permute-start.48) | collective-permute-done | bytes 7712 | tf_op jit(solution)/shard_map/ppermute | solution.py:781
  283.4 3.2 %collective-permute-start.55 = (bf16[96,768]{1,0:T(8,128)(2,1)S(1)}, bf16[96,768]{1,0:T(8,128)(2,1)S(1)}, u32[]{:S(2)}, u32[]{:S(2)}) collective-permute-start(bf16[96,768]{1,0:T(8,128)(2,1)S(1)} %copy-done.56), channel_id=1, source_target_pairs={{0,24},{1,25},{2,26},{3,27},{4,28},{5,29},{6,30},{7,31},{8,16},{9,... | collective-permute-start | bytes 442376 | tf_op jit(solution)/shard_map/ppermute | solution.py:781
  286.6 7.7 %output.3 = bf16[1024,768]{1,0:T(8,128)(2,1)} custom-call(bf16[1024,768]{1,0:T(8,128)(2,1)} %get-tuple-element.210.refs_0_, bf16[1024,768]{1,0:T(8,128)(2,1)} %get-tuple-element.211.refs_1_, bf16[192,768]{1,0:T(8,128)(2,1)} %copy-done.4, bf16[192,768]{1,0:T(8,128)(2,1)} %copy-done.8, bf16[192,768]{1,0:T(8,128)(2,1)} %copy-done.10, ...), custom_call_target="tpu_custom_call" | custom-call | flops 2415919104 | bytes 12000000 | tf_op jit(solution)/shard_map/output/pallas_call | solution.py:710
  294.3 1.9 collective-permute-done.54
  296.3 1.7 collective-permute-start.58
  298.0 2.7 collective-permute-start.57
  300.9 2.4 multiply_add_fusion
  (272 shorter events, 47.7 us)
Async XLA Ops:
  1.9 18.2 %collective-permute-start.2 = (bf16[96,768]{1,0:T(8,128)(2,1)S(1)}, bf16[96,768]{1,0:T(8,128)(2,1)S(1)}, u32[]{:S(2)}, u32[]{:S(2)}) collective-permute-start(bf16[96,768]{1,0:T(8,128)(2,1)S(1)} %slice_bitcast_fusion.16), channel_id=1, source_target_pairs={{0,24},{1,25},{2,26},{3,27},{4,28},{5,29},{6,30},{7,31},{8,16},{9,... | collective-permute-start | bytes 442376 | tf_op jit(solution)/shard_map/ppermute | solution.py:781
  7.0 12.5 %collective-permute-start.1 = (bf16[96,768]{1,0:T(8,128)(2,1)S(1)}, bf16[96,768]{1,0:T(8,128)(2,1)S(1)}, u32[]{:S(2)}, u32[]{:S(2)}) collective-permute-start(bf16[96,768]{1,0:T(8,128)(2,1)S(1)} %slice_bitcast_fusion.16), channel_id=1, source_target_pairs={{0,16},{1,17},{2,18},{3,19},{4,20},{5,21},{6,22},{7,23},{8,24},{9,... | collective-permute-start | bytes 442376 | tf_op jit(solution)/shard_map/ppermute | solution.py:781
  7.0 9.5 %collective-permute-start = (bf16[96,768]{1,0:T(8,128)(2,1)S(1)}, bf16[96,768]{1,0:T(8,128)(2,1)S(1)}, u32[]{:S(2)}, u32[]{:S(2)}) collective-permute-start(bf16[96,768]{1,0:T(8,128)(2,1)S(1)} %slice_bitcast_fusion.16), channel_id=1, source_target_pairs={{0,8},{1,9},{2,10},{3,11},{4,12},{5,13},{6,14},{7,15},{8,0},{9,1},... | collective-permute-start | bytes 442376 | tf_op jit(solution)/shard_map/ppermute | solution.py:781
  20.8 8.1 %collective-permute-start.8 = (bf16[192,768]{1,0:T(8,128)(2,1)S(1)}, bf16[192,768]{1,0:T(8,128)(2,1)S(1)}, u32[]{:S(2)}, u32[]{:S(2)}) collective-permute-start(bf16[192,768]{1,0:T(8,128)(2,1)S(1)} %pad_maximum_fusion.2), channel_id=1, source_target_pairs={{0,2},{1,3},{2,0},{3,1},{4,6},{5,7},{6,4},{7,5},{8,10},{9,11},{10,... | collective-permute-start | bytes 884744 | tf_op jit(solution)/shard_map/ppermute | solution.py:781
  22.4 8.2 %collective-permute-start.6 = (bf16[192,768]{1,0:T(8,128)(2,1)S(1)}, bf16[192,768]{1,0:T(8,128)(2,1)S(1)}, u32[]{:S(2)}, u32[]{:S(2)}) collective-permute-start(bf16[192,768]{1,0:T(8,128)(2,1)S(1)} %pad_maximum_fusion.1), channel_id=1, source_target_pairs={{0,4},{1,5},{2,6},{3,7},{4,0},{5,1},{6,2},{7,3},{8,12},{9,13},{10,... | collective-permute-start | bytes 884744 | tf_op jit(solution)/shard_map/ppermute | solution.py:781
  24.1 15.0 %collective-permute-start.5 = (bf16[192,768]{1,0:T(8,128)(2,1)S(1)}, bf16[192,768]{1,0:T(8,128)(2,1)S(1)}, u32[]{:S(2)}, u32[]{:S(2)}) collective-permute-start(bf16[192,768]{1,0:T(8,128)(2,1)S(1)} %pad_maximum_fusion), channel_id=1, source_target_pairs={{0,24},{1,25},{2,26},{3,27},{4,28},{5,29},{6,30},{7,31},{8,16},{9,... | collective-permute-start | bytes 884744 | tf_op jit(solution)/shard_map/ppermute | solution.py:781
  29.0 14.0 %collective-permute-start.9 = (bf16[384,768]{1,0:T(8,128)(2,1)S(1)}, bf16[384,768]{1,0:T(8,128)(2,1)}, u32[]{:S(2)}, u32[]{:S(2)}) collective-permute-start(bf16[384,768]{1,0:T(8,128)(2,1)S(1)} %constant_dynamic-update-slice_fusion.5.refs_2_), channel_id=1, source_target_pairs={{0,4},{1,5},{2,6},{3,7},{4,0},{5,1},{6,2},{7,3},{8,12},{9,13},{10,... | collective-permute-start | bytes 1769480 | tf_op jit(solution)/shard_map/ppermute | solution.py:781
  31.3 13.4 %collective-permute-start.7 = (bf16[384,768]{1,0:T(8,128)(2,1)}, bf16[384,768]{1,0:T(8,128)(2,1)}, u32[]{:S(2)}, u32[]{:S(2)}) collective-permute-start(bf16[384,768]{1,0:T(8,128)(2,1)} %constant_dynamic-update-slice_fusion.refs_0_), channel_id=1, source_target_pairs={{0,2},{1,3},{2,0},{3,1},{4,6},{5,7},{6,4},{7,5},{8,10},{9,11},{10,... | collective-permute-start | bytes 1769480 | tf_op jit(solution)/shard_map/ppermute | solution.py:781
  36.1 14.0 %collective-permute-start.4 = (bf16[192,768]{1,0:T(8,128)(2,1)S(1)}, bf16[192,768]{1,0:T(8,128)(2,1)S(1)}, u32[]{:S(2)}, u32[]{:S(2)}) collective-permute-start(bf16[192,768]{1,0:T(8,128)(2,1)S(1)} %pad_maximum_fusion), channel_id=1, source_target_pairs={{0,16},{1,17},{2,18},{3,19},{4,20},{5,21},{6,22},{7,23},{8,24},{9,... | collective-permute-start | bytes 884744 | tf_op jit(solution)/shard_map/ppermute | solution.py:781
  36.1 14.0 %collective-permute-start.3 = (bf16[192,768]{1,0:T(8,128)(2,1)S(1)}, bf16[192,768]{1,0:T(8,128)(2,1)S(1)}, u32[]{:S(2)}, u32[]{:S(2)}) collective-permute-start(bf16[192,768]{1,0:T(8,128)(2,1)S(1)} %pad_maximum_fusion), channel_id=1, source_target_pairs={{0,8},{1,9},{2,10},{3,11},{4,12},{5,13},{6,14},{7,15},{8,0},{9,1},... | collective-permute-start | bytes 884744 | tf_op jit(solution)/shard_map/ppermute | solution.py:781
  44.8 8.2 %collective-permute-start.15 = (bf16[384,768]{1,0:T(8,128)(2,1)S(1)}, bf16[384,768]{1,0:T(8,128)(2,1)S(1)}, u32[]{:S(2)}, u32[]{:S(2)}) collective-permute-start(bf16[384,768]{1,0:T(8,128)(2,1)S(1)} %constant_dynamic-update-slice_fusion.5.refs_2_), channel_id=1, source_target_pairs={{0,1},{1,0},{2,3},{3,2},{4,5},{5,4},{6,7},{7,6},{8,9},{9,8},{10,11... | collective-permute-start | bytes 1769480 | tf_op jit(solution)/shard_map/ppermute | solution.py:781
  50.3 23.0 %collective-permute-start.11 = (bf16[192,768]{1,0:T(8,128)(2,1)S(1)}, bf16[192,768]{1,0:T(8,128)(2,1)S(1)}, u32[]{:S(2)}, u32[]{:S(2)}) collective-permute-start(bf16[192,768]{1,0:T(8,128)(2,1)S(1)} %get-tuple-element.119.refs_0_), channel_id=1, source_target_pairs={{0,4},{1,5},{2,6},{3,7},{4,0},{5,1},{6,2},{7,3},{8,12},{9,13},{10,... | collective-permute-start | bytes 884744 | tf_op jit(solution)/shard_map/ppermute | solution.py:781
  50.9 40.8 %collective-permute-start.10 = (bf16[192,768]{1,0:T(8,128)(2,1)S(1)}, bf16[192,768]{1,0:T(8,128)(2,1)S(1)}, u32[]{:S(2)}, u32[]{:S(2)}) collective-permute-start(bf16[192,768]{1,0:T(8,128)(2,1)S(1)} %get-tuple-element.119.refs_0_), channel_id=1, source_target_pairs={{0,2},{1,3},{2,0},{3,1},{4,6},{5,7},{6,4},{7,5},{8,10},{9,11},{10,... | collective-permute-start | bytes 884744 | tf_op jit(solution)/shard_map/ppermute | solution.py:781
  51.7 21.6 %collective-permute-start.12 = (bf16[192,768]{1,0:T(8,128)(2,1)S(1)}, bf16[192,768]{1,0:T(8,128)(2,1)S(1)}, u32[]{:S(2)}, u32[]{:S(2)}) collective-permute-start(bf16[192,768]{1,0:T(8,128)(2,1)S(1)} %get-tuple-element.120.refs_4_.refs_2_), channel_id=1, source_target_pairs={{0,2},{1,3},{2,0},{3,1},{4,6},{5,7},{6,4},{7,5},{8,10},{9,11},{10,... | collective-permute-start | bytes 884744 | tf_op jit(solution)/shard_map/ppermute | solution.py:781
  52.9 18.0 %collective-permute-start.20 = (bf16[192,768]{1,0:T(8,128)(2,1)S(1)}, bf16[192,768]{1,0:T(8,128)(2,1)S(1)}, u32[]{:S(2)}, u32[]{:S(2)}) collective-permute-start(bf16[192,768]{1,0:T(8,128)(2,1)S(1)} %get-tuple-element.149.refs_0_), channel_id=1, source_target_pairs={{0,4},{1,5},{2,6},{3,7},{4,0},{5,1},{6,2},{7,3},{8,12},{9,13},{10,... | collective-permute-start | bytes 884744 | tf_op jit(solution)/shard_map/ppermute | solution.py:781
  54.4 18.8 %collective-permute-start.21 = (bf16[192,768]{1,0:T(8,128)(2,1)S(1)}, bf16[192,768]{1,0:T(8,128)(2,1)S(1)}, u32[]{:S(2)}, u32[]{:S(2)}) collective-permute-start(bf16[192,768]{1,0:T(8,128)(2,1)S(1)} %get-tuple-element.150.refs_4_.refs_6_), channel_id=1, source_target_pairs={{0,2},{1,3},{2,0},{3,1},{4,6},{5,7},{6,4},{7,5},{8,10},{9,11},{10,... | collective-permute-start | bytes 884744 | tf_op jit(solution)/shard_map/ppermute | solution.py:781
  71.0 20.7 %collective-permute-start.18 = (bf16[192,768]{1,0:T(8,128)(2,1)S(1)}, bf16[192,768]{1,0:T(8,128)(2,1)S(1)}, u32[]{:S(2)}, u32[]{:S(2)}) collective-permute-start(bf16[192,768]{1,0:T(8,128)(2,1)S(1)} %get-tuple-element.120.refs_4_.refs_2_), channel_id=1, source_target_pairs={{0,4},{1,5},{2,6},{3,7},{4,0},{5,1},{6,2},{7,3},{8,12},{9,13},{10,... | collective-permute-start | bytes 884744 | tf_op jit(solution)/shard_map/ppermute | solution.py:781
  73.3 18.4 %collective-permute-start.17 = (bf16[192,768]{1,0:T(8,128)(2,1)S(1)}, bf16[192,768]{1,0:T(8,128)(2,1)S(1)}, u32[]{:S(2)}, u32[]{:S(2)}) collective-permute-start(bf16[192,768]{1,0:T(8,128)(2,1)S(1)} %collective-permute-done.11.refs_2_), channel_id=1, source_target_pairs={{0,2},{1,3},{2,0},{3,1},{4,6},{5,7},{6,4},{7,5},{8,10},{9,11},{10,... | collective-permute-start | bytes 884744 | tf_op jit(solution)/shard_map/ppermute | solution.py:781
  75.6 16.2 %collective-permute-start.19 = (bf16[192,768]{1,0:T(8,128)(2,1)S(1)}, bf16[192,768]{1,0:T(8,128)(2,1)S(1)}, u32[]{:S(2)}, u32[]{:S(2)}) collective-permute-start(bf16[192,768]{1,0:T(8,128)(2,1)S(1)} %collective-permute-done.12.refs_5_.refs_3_), channel_id=1, source_target_pairs={{0,4},{1,5},{2,6},{3,7},{4,0},{5,1},{6,2},{7,3},{8,12},{9,13},{10,... | collective-permute-start | bytes 884744 | tf_op jit(solution)/shard_map/ppermute | solution.py:781
  77.6 19.0 %collective-permute-start.23 = (bf16[1024,768]{1,0:T(8,128)(2,1)S(1)}, bf16[1024,768]{1,0:T(8,128)(2,1)S(1)}, u32[]{:S(2)}, u32[]{:S(2)}) collective-permute-start(bf16[1024,768]{1,0:T(8,128)(2,1)S(1)} %copy-done.44), channel_id=1, source_target_pairs={{0,1},{1,0},{2,3},{3,2},{4,5},{5,4},{6,7},{7,6},{8,9},{9,8},{10,11... | collective-permute-start | bytes 4718600 | tf_op jit(solution)/shard_map/ppermute | solution.py:781
  94.4 34.0 %collective-permute-start.25 = (bf16[192,768]{1,0:T(8,128)(2,1)S(1)}, bf16[192,768]{1,0:T(8,128)(2,1)S(1)}, u32[]{:S(2)}, u32[]{:S(2)}) collective-permute-start(bf16[192,768]{1,0:T(8,128)(2,1)S(1)} %collective-permute-done.20.refs_2_), channel_id=1, source_target_pairs={{0,2},{1,3},{2,0},{3,1},{4,6},{5,7},{6,4},{7,5},{8,10},{9,11},{10,... | collective-permute-start | bytes 884744 | tf_op jit(solution)/shard_map/ppermute | solution.py:781
  95.7 32.7 %collective-permute-start.27 = (bf16[192,768]{1,0:T(8,128)(2,1)S(1)}, bf16[192,768]{1,0:T(8,128)(2,1)S(1)}, u32[]{:S(2)}, u32[]{:S(2)}) collective-permute-start(bf16[192,768]{1,0:T(8,128)(2,1)S(1)} %collective-permute-done.21.refs_5_.refs_7_), channel_id=1, source_target_pairs={{0,4},{1,5},{2,6},{3,7},{4,0},{5,1},{6,2},{7,3},{8,12},{9,13},{10,... | collective-permute-start | bytes 884744 | tf_op jit(solution)/shard_map/ppermute | solution.py:781
  95.7 32.7 %collective-permute-start.24 = (bf16[192,768]{1,0:T(8,128)(2,1)S(1)}, bf16[192,768]{1,0:T(8,128)(2,1)}, u32[]{:S(2)}, u32[]{:S(2)}) collective-permute-start(bf16[192,768]{1,0:T(8,128)(2,1)S(1)} %get-tuple-element.149.refs_0_), channel_id=1, source_target_pairs={{0,2},{1,3},{2,0},{3,1},{4,6},{5,7},{6,4},{7,5},{8,10},{9,11},{10,... | collective-permute-start | bytes 884744 | tf_op jit(solution)/shard_map/ppermute | solution.py:781
  96.5 31.9 %collective-permute-start.26 = (bf16[192,768]{1,0:T(8,128)(2,1)S(1)}, bf16[192,768]{1,0:T(8,128)(2,1)S(1)}, u32[]{:S(2)}, u32[]{:S(2)}) collective-permute-start(bf16[192,768]{1,0:T(8,128)(2,1)S(1)} %get-tuple-element.150.refs_4_.refs_6_), channel_id=1, source_target_pairs={{0,4},{1,5},{2,6},{3,7},{4,0},{5,1},{6,2},{7,3},{8,12},{9,13},{10,... | collective-permute-start | bytes 884744 | tf_op jit(solution)/shard_map/ppermute | solution.py:781
  138.1 29.9 %collective-permute-start.30 = (f32[1024,768]{1,0:T(8,128)}, f32[1024,768]{1,0:T(8,128)}, u32[]{:S(2)}, u32[]{:S(2)}) collective-permute-start(f32[1024,768]{1,0:T(8,128)} %get-tuple-element.166), channel_id=1, source_target_pairs={{0,1},{1,0},{2,3},{3,2},{4,5},{5,4},{6,7},{7,6},{8,9},{9,8},{10,11... | collective-permute-start | bytes 9437192 | tf_op jit(solution)/shard_map/ppermute | solution.py:781
  138.1 25.0 %collective-permute-start.28 = (bf16[2,4,48,768]{3,2,1,0:T(8,128)(2,1)S(1)}, bf16[2,4,48,768]{3,2,1,0:T(8,128)(2,1)}, u32[]{:S(2)}, u32[]{:S(2)}) collective-permute-start(bf16[2,4,48,768]{3,2,1,0:T(8,128)(2,1)S(1)} %slice_bitcast_fusion.15), channel_id=1, source_target_pairs={{0,2},{1,3},{2,0},{3,1},{4,6},{5,7},{6,4},{7,5},{8,10},{9,11},{10,... | collective-permute-start | bytes 1769480 | tf_op jit(solution)/shard_map/ppermute | solution.py:781
  139.5 23.6 %collective-permute-start.29 = (bf16[2,4,48,768]{3,2,1,0:T(8,128)(2,1)S(1)}, bf16[2,4,48,768]{3,2,1,0:T(8,128)(2,1)}, u32[]{:S(2)}, u32[]{:S(2)}) collective-permute-start(bf16[2,4,48,768]{3,2,1,0:T(8,128)(2,1)S(1)} %slice_bitcast_fusion.14), channel_id=1, source_target_pairs={{0,4},{1,5},{2,6},{3,7},{4,0},{5,1},{6,2},{7,3},{8,12},{9,13},{10,... | collective-permute-start | bytes 1769480 | tf_op jit(solution)/shard_map/ppermute | solution.py:781
  159.9 34.3 %collective-permute-start.33 = (bf16[2,4,48,768]{3,2,1,0:T(8,128)(2,1)S(1)}, bf16[2,4,48,768]{3,2,1,0:T(8,128)(2,1)S(1)}, u32[]{:S(2)}, u32[]{:S(2)}) collective-permute-start(bf16[2,4,48,768]{3,2,1,0:T(8,128)(2,1)S(1)} %slice_bitcast_fusion.11), channel_id=1, source_target_pairs={{0,2},{1,3},{2,0},{3,1},{4,6},{5,7},{6,4},{7,5},{8,10},{9,11},{10,... | collective-permute-start | bytes 1769480 | tf_op jit(solution)/shard_map/ppermute | solution.py:781
  162.1 32.2 %collective-permute-start.34 = (bf16[2,4,48,768]{3,2,1,0:T(8,128)(2,1)S(1)}, bf16[2,4,48,768]{3,2,1,0:T(8,128)(2,1)S(1)}, u32[]{:S(2)}, u32[]{:S(2)}) collective-permute-start(bf16[2,4,48,768]{3,2,1,0:T(8,128)(2,1)S(1)} %slice_bitcast_fusion.10), channel_id=1, source_target_pairs={{0,4},{1,5},{2,6},{3,7},{4,0},{5,1},{6,2},{7,3},{8,12},{9,13},{10,... | collective-permute-start | bytes 1769480 | tf_op jit(solution)/shard_map/ppermute | solution.py:781
  165.6 28.6 %collective-permute-start.32 = (bf16[4,48,768]{2,1,0:T(8,128)(2,1)S(1)}, bf16[4,48,768]{2,1,0:T(8,128)(2,1)S(1)}, u32[]{:S(2)}, u32[]{:S(2)}) collective-permute-start(bf16[4,48,768]{2,1,0:T(8,128)(2,1)S(1)} %get-tuple-element.271), channel_id=1, source_target_pairs={{0,2},{1,3},{2,0},{3,1},{4,6},{5,7},{6,4},{7,5},{8,10},{9,11},{10,... | collective-permute-start | bytes 884744 | tf_op jit(solution)/shard_map/ppermute | solution.py:781
  166.9 27.4 %collective-permute-start.31 = (bf16[4,48,768]{2,1,0:T(8,128)(2,1)S(1)}, bf16[4,48,768]{2,1,0:T(8,128)(2,1)S(1)}, u32[]{:S(2)}, u32[]{:S(2)}) collective-permute-start(bf16[4,48,768]{2,1,0:T(8,128)(2,1)S(1)} %get-tuple-element.276), channel_id=1, source_target_pairs={{0,4},{1,5},{2,6},{3,7},{4,0},{5,1},{6,2},{7,3},{8,12},{9,13},{10,... | collective-permute-start | bytes 884744 | tf_op jit(solution)/shard_map/ppermute | solution.py:781
  197.4 32.6 %collective-permute-start.35 = (bf16[96,768]{1,0:T(8,128)(2,1)}, bf16[96,768]{1,0:T(8,128)(2,1)S(1)}, u32[]{:S(2)}, u32[]{:S(2)}) collective-permute-start(bf16[96,768]{1,0:T(8,128)(2,1)} %get-tuple-element.174), channel_id=1, source_target_pairs={{0,8},{1,9},{2,10},{3,11},{4,12},{5,13},{6,14},{7,15},{8,0},{9,1},... | collective-permute-start | bytes 442376 | tf_op jit(solution)/shard_map/ppermute | solution.py:781
  197.4 32.6 %collective-permute-start.36 = (bf16[96,768]{1,0:T(8,128)(2,1)}, bf16[96,768]{1,0:T(8,128)(2,1)S(1)}, u32[]{:S(2)}, u32[]{:S(2)}) collective-permute-start(bf16[96,768]{1,0:T(8,128)(2,1)} %get-tuple-element.175), channel_id=1, source_target_pairs={{0,16},{1,17},{2,18},{3,19},{4,20},{5,21},{6,22},{7,23},{8,24},{9,... | collective-permute-start | bytes 442376 | tf_op jit(solution)/shard_map/ppermute | solution.py:781
  200.3 29.7 %collective-permute-start.37 = (bf16[96,768]{1,0:T(8,128)(2,1)}, bf16[96,768]{1,0:T(8,128)(2,1)S(1)}, u32[]{:S(2)}, u32[]{:S(2)}) collective-permute-start(bf16[96,768]{1,0:T(8,128)(2,1)} %get-tuple-element.176), channel_id=1, source_target_pairs={{0,24},{1,25},{2,26},{3,27},{4,28},{5,29},{6,30},{7,31},{8,16},{9,... | collective-permute-start | bytes 442376 | tf_op jit(solution)/shard_map/ppermute | solution.py:781
  203.0 26.9 %collective-permute-start.39 = (bf16[4,48,768]{2,1,0:T(8,128)(2,1)S(1)}, bf16[4,48,768]{2,1,0:T(8,128)(2,1)S(1)}, u32[]{:S(2)}, u32[]{:S(2)}) collective-permute-start(bf16[4,48,768]{2,1,0:T(8,128)(2,1)S(1)} %get-tuple-element.267), channel_id=1, source_target_pairs={{0,2},{1,3},{2,0},{3,1},{4,6},{5,7},{6,4},{7,5},{8,10},{9,11},{10,... | collective-permute-start | bytes 884744 | tf_op jit(solution)/shard_map/ppermute | solution.py:781
  211.0 19.0 %collective-permute-start.38 = (bf16[4,48,768]{2,1,0:T(8,128)(2,1)S(1)}, bf16[4,48,768]{2,1,0:T(8,128)(2,1)S(1)}, u32[]{:S(2)}, u32[]{:S(2)}) collective-permute-start(bf16[4,48,768]{2,1,0:T(8,128)(2,1)S(1)} %get-tuple-element.274), channel_id=1, source_target_pairs={{0,4},{1,5},{2,6},{3,7},{4,0},{5,1},{6,2},{7,3},{8,12},{9,13},{10,... | collective-permute-start | bytes 884744 | tf_op jit(solution)/shard_map/ppermute | solution.py:781
  238.3 19.1 %collective-permute-start.41 = (bf16[2,4,48,768]{3,2,1,0:T(8,128)(2,1)}, bf16[2,4,48,768]{3,2,1,0:T(8,128)(2,1)S(1)}, u32[]{:S(2)}, u32[]{:S(2)}) collective-permute-start(bf16[2,4,48,768]{3,2,1,0:T(8,128)(2,1)} %get-tuple-element.264), channel_id=1, source_target_pairs={{0,2},{1,3},{2,0},{3,1},{4,6},{5,7},{6,4},{7,5},{8,10},{9,11},{10,... | collective-permute-start | bytes 1769480 | tf_op jit(solution)/shard_map/ppermute | solution.py:781
  241.9 15.6 %collective-permute-start.42 = (bf16[2,4,48,768]{3,2,1,0:T(8,128)(2,1)S(1)}, bf16[2,4,48,768]{3,2,1,0:T(8,128)(2,1)}, u32[]{:S(2)}, u32[]{:S(2)}) collective-permute-start(bf16[2,4,48,768]{3,2,1,0:T(8,128)(2,1)S(1)} %get-tuple-element.263), channel_id=1, source_target_pairs={{0,4},{1,5},{2,6},{3,7},{4,0},{5,1},{6,2},{7,3},{8,12},{9,13},{10,... | collective-permute-start | bytes 1769480 | tf_op jit(solution)/shard_map/ppermute | solution.py:781
  243.2 19.9 %collective-permute-start.43 = (bf16[96,768]{1,0:T(8,128)(2,1)}, bf16[96,768]{1,0:T(8,128)(2,1)}, u32[]{:S(2)}, u32[]{:S(2)}) collective-permute-start(bf16[96,768]{1,0:T(8,128)(2,1)} %get-tuple-element.186), channel_id=1, source_target_pairs={{0,8},{1,9},{2,10},{3,11},{4,12},{5,13},{6,14},{7,15},{8,0},{9,1},... | collective-permute-start | bytes 442376 | tf_op jit(solution)/shard_map/ppermute | solution.py:781
  243.3 19.8 %collective-permute-start.44 = (bf16[96,768]{1,0:T(8,128)(2,1)}, bf16[96,768]{1,0:T(8,128)(2,1)}, u32[]{:S(2)}, u32[]{:S(2)}) collective-permute-start(bf16[96,768]{1,0:T(8,128)(2,1)} %get-tuple-element.187), channel_id=1, source_target_pairs={{0,16},{1,17},{2,18},{3,19},{4,20},{5,21},{6,22},{7,23},{8,24},{9,... | collective-permute-start | bytes 442376 | tf_op jit(solution)/shard_map/ppermute | solution.py:781
  243.9 19.2 %collective-permute-start.45 = (bf16[96,768]{1,0:T(8,128)(2,1)}, bf16[96,768]{1,0:T(8,128)(2,1)}, u32[]{:S(2)}, u32[]{:S(2)}) collective-permute-start(bf16[96,768]{1,0:T(8,128)(2,1)} %get-tuple-element.188), channel_id=1, source_target_pairs={{0,24},{1,25},{2,26},{3,27},{4,28},{5,29},{6,30},{7,31},{8,16},{9,... | collective-permute-start | bytes 442376 | tf_op jit(solution)/shard_map/ppermute | solution.py:781
  259.5 10.6 %collective-permute-start.47 = (bf16[4,48,768]{2,1,0:T(8,128)(2,1)S(1)}, bf16[4,48,768]{2,1,0:T(8,128)(2,1)S(1)}, u32[]{:S(2)}, u32[]{:S(2)}) collective-permute-start(bf16[4,48,768]{2,1,0:T(8,128)(2,1)S(1)} %get-tuple-element.279), channel_id=1, source_target_pairs={{0,2},{1,3},{2,0},{3,1},{4,6},{5,7},{6,4},{7,5},{8,10},{9,11},{10,... | collective-permute-start | bytes 884744 | tf_op jit(solution)/shard_map/ppermute | solution.py:781
  273.2 10.2 %collective-permute-start.49 = (f32[1024,768]{1,0:T(8,128)}, f32[1024,768]{1,0:T(8,128)S(1)}, u32[]{:S(2)}, u32[]{:S(2)}) collective-permute-start(f32[1024,768]{1,0:T(8,128)} %output.2), channel_id=1, source_target_pairs={{0,1},{1,0},{2,3},{3,2},{4,5},{5,4},{6,7},{7,6},{8,9},{9,8},{10,11... | collective-permute-start | bytes 9437192 | tf_op jit(solution)/shard_map/ppermute | solution.py:781
  279.9 14.5 %collective-permute-start.51 = (f32[15,128]{1,0:T(8,128)S(1)}, f32[15,128]{1,0:T(8,128)S(1)}, u32[]{:S(2)}, u32[]{:S(2)}) collective-permute-start(f32[15,128]{1,0:T(8,128)S(1)} %fusion.41), channel_id=1, source_target_pairs={{0,4},{1,5},{2,6},{3,7},{4,0},{5,1},{6,2},{7,3},{8,12},{9,13},{10,... | collective-permute-start | bytes 23048 | tf_op jit(solution)/shard_map/ppermute | solution.py:781
  281.3 13.0 %collective-permute-start.50 = (f32[15,128]{1,0:T(8,128)S(1)}, f32[15,128]{1,0:T(8,128)S(1)}, u32[]{:S(2)}, u32[]{:S(2)}) collective-permute-start(f32[15,128]{1,0:T(8,128)S(1)} %fusion.41), channel_id=1, source_target_pairs={{0,2},{1,3},{2,0},{3,1},{4,6},{5,7},{6,4},{7,5},{8,10},{9,11},{10,... | collective-permute-start | bytes 23048 | tf_op jit(solution)/shard_map/ppermute | solution.py:781
  282.1 12.2 %collective-permute-start.53 = (bf16[96,768]{1,0:T(8,128)(2,1)}, bf16[96,768]{1,0:T(8,128)(2,1)S(1)}, u32[]{:S(2)}, u32[]{:S(2)}) collective-permute-start(bf16[96,768]{1,0:T(8,128)(2,1)} %get-tuple-element.205), channel_id=1, source_target_pairs={{0,8},{1,9},{2,10},{3,11},{4,12},{5,13},{6,14},{7,15},{8,0},{9,1},... | collective-permute-start | bytes 442376 | tf_op jit(solution)/shard_map/ppermute | solution.py:781
  283.0 13.2 %collective-permute-start.54 = (bf16[96,768]{1,0:T(8,128)(2,1)}, bf16[96,768]{1,0:T(8,128)(2,1)S(1)}, u32[]{:S(2)}, u32[]{:S(2)}) collective-permute-start(bf16[96,768]{1,0:T(8,128)(2,1)} %get-tuple-element.206), channel_id=1, source_target_pairs={{0,16},{1,17},{2,18},{3,19},{4,20},{5,21},{6,22},{7,23},{8,24},{9,... | collective-permute-start | bytes 442376 | tf_op jit(solution)/shard_map/ppermute | solution.py:781
  283.4 12.9 %collective-permute-start.55 = (bf16[96,768]{1,0:T(8,128)(2,1)S(1)}, bf16[96,768]{1,0:T(8,128)(2,1)S(1)}, u32[]{:S(2)}, u32[]{:S(2)}) collective-permute-start(bf16[96,768]{1,0:T(8,128)(2,1)S(1)} %copy-done.56), channel_id=1, source_target_pairs={{0,24},{1,25},{2,26},{3,27},{4,28},{5,29},{6,30},{7,31},{8,16},{9,... | collective-permute-start | bytes 442376 | tf_op jit(solution)/shard_map/ppermute | solution.py:781
  (75 other events, 766.2 us)
